TPU v7x, 128 devices: a whole 4x4x4 slice. The times are simulated.
128 devices in a mesh: pool: 16 (over y, z), head: 8 (over x, core).
Axes of the slice: x: 4, y: 4, z: 4, core: 2. Of those that a mesh axis runs over, the one named last changes fastest.
Arguments:
- hidden: bfloat16 [16, 256, 5120], P('pool', None, 'head'), may hold values from -6 to 6
- snap_map: int32 [16], replicated, may hold values from 0 to 127
- pool_states: bfloat16 [128, 64, 64, 256], P('pool', 'head'), may hold values from -2.390625 to 2.390625
- w_zx: bfloat16 [5120, 2, 4096], P('pool', None, 'head'), may hold values from -0.078125 to 0.078125
- w_bc: bfloat16 [5120, 512], P('pool'), may hold values from -0.078125 to 0.078125
- w_dt: bfloat16 [5120, 64], P('pool', 'head'), may hold values from -0.078125 to 0.078125
- dt_bias: float32 [64], P('head'), may hold values from -6 to -2
- decay_rate: float32 [64], P('head'), may hold values from 0.05 to 2
- skip: float32 [64], P('head'), may hold values from 0.5 to 2
- norm_gain: float32 [4096], P('head'), may hold values from 0.1 to 1.9
- w_out: bfloat16 [4096, 5120], P('head', 'pool'), may hold values from -0.09375 to 0.09375
Outputs:
- mixed: bfloat16 [16, 256, 5120], P('pool', None, 'head')
- final_state: float32 [16, 64, 64, 256], P('pool', 'head')
All inputs are finite; a program needn't handle non-finite values.
Results may differ from a plain program's by a relative error of at most 0.018.
Values may be sent and summed in bfloat16 or wider, within the bound.
A program may use at most 128 MiB of HBM per device.

v0:
```python
import jax
import jax.numpy as jnp
from jax import lax
from jax.sharding import PartitionSpec as P

SPAN = 256


def span_scan(values, steps_dt, bmat, cmat, rate, start_state):
    highest = lax.Precision.HIGHEST
    tokens_n, heads_n, head_dim = values.shape
    state_dim = bmat.shape[1]
    spans = tokens_n // SPAN
    cumlog = jnp.cumsum((-(rate[None, :] * steps_dt)).reshape(spans, SPAN, heads_n), axis=1)
    lower = (jnp.arange(SPAN)[:, None] >= jnp.arange(SPAN)[None, :])[None, :, :, None]
    spread = jnp.where(lower, cumlog[:, :, None, :] - cumlog[:, None, :, :], 0.0)
    decays = jnp.where(lower, jnp.exp(spread), 0.0)
    bsplit = bmat.reshape(spans, SPAN, state_dim)
    csplit = cmat.reshape(spans, SPAN, state_dim)
    scores = jnp.einsum("kin,kjn->kij", csplit, bsplit, precision=highest)
    weighted = (values * steps_dt[:, :, None]).reshape(spans, SPAN, heads_n, head_dim)
    within = jnp.einsum(
        "kijh,kjhp->kihp", scores[:, :, :, None] * decays, weighted, precision=highest
    )
    tail_decay = jnp.exp(cumlog[:, -1:, :] - cumlog)
    states = jnp.einsum(
        "kjhp,kjn->khpn", weighted * tail_decay[:, :, :, None], bsplit, precision=highest
    )
    span_decay = jnp.exp(cumlog[:, -1, :])

    def advance(carry, items):
        factor, added = items
        return (factor[:, None, None] * carry + added, carry)

    final, starts = lax.scan(advance, start_state, (span_decay, states))
    carried = jnp.exp(cumlog)[:, :, :, None] * jnp.einsum(
        "kin,khpn->kihp", csplit, starts, precision=highest
    )
    return ((within + carried).reshape(tokens_n, heads_n, head_dim), final, cumlog)


def one_request(gate_part, inputs, maps, steps_dt, start_state, decay_rate, skip, norm_gain):
    length = inputs.shape[0]
    heads_here = steps_dt.shape[1]
    head_dim = inputs.shape[1] // heads_here
    state_dim = maps.shape[1] // 2
    values = inputs.astype(jnp.float32).reshape(length, heads_here, head_dim)
    bmat = maps[:, :state_dim].astype(jnp.float32)
    cmat = maps[:, state_dim:].astype(jnp.float32)
    scanned, final, cumlog = span_scan(values, steps_dt, bmat, cmat, decay_rate, start_state)
    gate_vals = gate_part.astype(jnp.float32).reshape(length, heads_here, head_dim)
    gated = (scanned + skip[None, :, None] * values) * jax.nn.silu(gate_vals)
    meansq = jnp.mean(gated * gated, axis=-1, keepdims=True)
    normed = gated * lax.rsqrt(meansq + 1e-05) * norm_gain.reshape(heads_here, head_dim)[None, :, :]
    return (normed.reshape(length, heads_here * head_dim).astype(jnp.bfloat16), final)


def shards(
    hidden, snap_map, pool_states, w_zx, w_bc, w_dt, dt_bias, decay_rate, skip, norm_gain, w_out
):
    reqs, length, _ = hidden.shape
    snap_dev, heads_here, head_dim, state_dim = pool_states.shape
    inner_here = heads_here * head_dim
    first = lax.axis_index("pool") * snap_dev
    onehot = (snap_map[:, None] == first + jnp.arange(snap_dev, dtype=jnp.int32)[None, :]).astype(
        jnp.bfloat16
    )
    cached = lax.psum_scatter(
        jnp.dot(
            onehot, pool_states.reshape(snap_dev, -1), preferred_element_type=jnp.float32
        ).astype(jnp.bfloat16),
        "pool",
        scatter_dimension=0,
        tiled=True,
    ).astype(jnp.float32)
    cached = cached.reshape(reqs, heads_here, head_dim, state_dim)
    whole = lax.all_gather(hidden, "head", axis=2, tiled=True)
    flat = whole.reshape(reqs * length, whole.shape[2])
    pieces = (
        lax.all_gather(w_zx, "pool", axis=0, tiled=True),
        lax.all_gather(w_bc, "pool", axis=0, tiled=True),
        lax.all_gather(w_dt, "pool", axis=0, tiled=True),
    )
    count = pieces[0].shape[0]
    proj_zx, proj_bc, proj_dt = tuple(
        (
            jnp.dot(flat, piece.reshape(count, -1), preferred_element_type=jnp.float32)
            for piece in pieces
        )
    )
    gate_part = proj_zx[:, :inner_here].astype(jnp.bfloat16)
    inputs = proj_zx[:, inner_here:].astype(jnp.bfloat16)
    maps = proj_bc.astype(jnp.bfloat16)
    steps_dt = jax.nn.softplus(proj_dt + dt_bias[None, :])
    normed, final_state = jax.vmap(one_request, in_axes=(0, 0, 0, 0, 0, None, None, None))(
        gate_part.reshape(reqs, length, inner_here),
        inputs.reshape(reqs, length, inner_here),
        maps.reshape(reqs, length, 2 * state_dim),
        steps_dt.reshape(reqs, length, heads_here),
        cached,
        decay_rate,
        skip,
        norm_gain,
    )
    flat_normed = normed.reshape(reqs * length, inner_here)
    terms = jnp.dot(
        flat_normed,
        lax.all_gather(w_out, "pool", axis=1, tiled=True),
        preferred_element_type=jnp.float32,
    )
    summed = lax.psum_scatter(
        terms.astype(jnp.bfloat16), "head", scatter_dimension=1, tiled=True
    ).astype(jnp.float32)
    return (summed.astype(jnp.bfloat16).reshape(reqs, length, summed.shape[1]), final_state)


def solution(mesh):
    in_specs = (
        P("pool", None, "head"),
        P(),
        P("pool", "head", None, None),
        P("pool", None, "head"),
        P("pool", None),
        P("pool", "head"),
        P("head"),
        P("head"),
        P("head"),
        P("head"),
        P("head", "pool"),
    )
    out_specs = (P("pool", None, "head"), P("pool", "head", None, None))
    return jax.shard_map(shards, mesh=mesh, in_specs=in_specs, out_specs=out_specs, check_vma=False)
```

profile of v0, /device:TPU:1, one launch (start us, length us, event | category | flops | bytes accessed | tf_op | source)
XLA Modules:
  0.0 309.6 jit_solution(7866505327791951998)
XLA Ops:
  8.1 2.8 copy.53
  10.8 3.3 %convolution_convert_fusion = bf16[16,131072]{1,0:T(8,128)(2,1)} fusion(bf16[8,131072]{1,0:T(8,128)(2,1)S(1)} %bitcast.112, s32[8]{0:T(128)S(1)} %iota_add_fusion, s32[16]{0:T(128)S(1)} %copy-done.9), kind=kOutput, calls=%fused_computation | convolution fusion | flops 35651712 | bytes 6291552 | tf_op jit(solution)/shard_map/dot_general | solution.py:69
  14.2 0.5 all-gather.6.cloned.1.call-update
  14.8 0.5 all-gather.10.cloned.1.call-update
  15.4 0.5 all-gather.8.cloned.1.call-update
  16.0 0.7 all-gather.12.cloned.1.call-update
  16.9 22.1 %all-gather = bf16[16,320,8]{1,2,0:T(8,128)(2,1)S(1)} all-gather(bf16[1,320,8]{1,2,0:T(8,128)(2,1)S(1)} %bitcast.124), channel_id=1, replica_groups=mesh['pool'=16,'head'=8] {'pool'}, dimensions={0}, use_global_device_ids=true | all-gather | bytes 87040 | tf_op jit(solution)/shard_map/all_gather | solution.py:82
  39.2 0.6 dynamic-slice
  39.8 107.0 %all-reduce.3.cloned.1.call-done = bf16[16,131072]{1,0:T(8,128)(2,1)} async-done(((bf16[16,131072]{1,0:T(8,128)(2,1)}), bf16[16,131072]{1,0:T(8,128)(2,1)}) %all-reduce.3.cloned.1.call-update) | async-done | bytes 4194320
  146.8 3.8 %dynamic-slice_reduce_fusion = bf16[131072]{0:T(1024)(128)(2,1)S(1)} fusion(bf16[16,131072]{1,0:T(8,128)(2,1)} %all-reduce.3.cloned.1.call-done, u32[]{:T(128)} %bitcast.37), kind=kLoop, calls=%fused_computation.29 | loop fusion | bytes 524292
  150.8 2.7 compare_select_fusion
  153.6 0.7 reduce-window.6
  154.6 4.0 %fusion.26 = bf16[1,256,512]{2,1,0:T(8,128)(2,1)S(1)} fusion(bf16[5120,512]{1,0:T(8,128)(2,1)} %all-gather.10.cloned.1.call-done, bf16[1,256,5120]{2,1,0:T(8,128)(2,1)S(1)} %copy-done), kind=kOutput, calls=%fused_computation.22 | convolution fusion | flops 1342308352 | bytes 8126464 | tf_op jit(solution)/shard_map/dot_general | solution.py:87
  158.7 1.1 fusion.18
  159.7 0.9 fusion.47
  160.6 42.6 %all-gather.8.cloned.1.call-done = bf16[5120,2,512]{2,1,0:T(2,128)(2,1)} async-done(((bf16[320,2,512]{2,1,0:T(2,128)(2,1)}), bf16[5120,2,512]{2,1,0:T(2,128)(2,1)}) %all-gather.8.cloned.1.call-update) | async-done | bytes 10485776 | tf_op jit(solution)/shard_map/all_gather | solution.py:80
  203.2 11.3 %copy.52 = bf16[640,8,2,512]{3,1,2,0:T(8,128)(2,1)} copy(bf16[640,8,2,512]{3,2,1,0:T(2,128)(2,1)} %bitcast.109) | data formatting | bytes 20971520
  214.5 7.0 %fusion.12 = bf16[256,1024]{1,0:T(8,128)(2,1)S(1)} fusion(bf16[5120,1024]{1,0:T(8,128)(2,1)} %bitcast.110, bf16[1,256,5120]{2,1,0:T(8,128)(2,1)S(1)} %copy-done), kind=kOutput, calls=%fused_computation.14 | convolution fusion | flops 2684616704 | bytes 13631488 | tf_op jit(solution)/shard_map/dot_general | solution.py:87
  221.7 0.2 copy.45
  221.9 0.2 copy.41
  222.1 0.5 copy-done.3
  222.7 2.5 fusion.39
  225.2 1.0 copy.43
  226.3 1.0 copy.46
  227.3 34.2 %all-gather.12.cloned.1.call-done = bf16[512,5120]{0,1:T(8,128)(2,1)} async-done(((bf16[512,320]{0,1:T(8,128)(2,1)}), bf16[512,5120]{0,1:T(8,128)(2,1)}) %all-gather.12.cloned.1.call-update) | async-done | bytes 5242896 | tf_op jit(solution)/shard_map/all_gather | solution.py:108
  261.5 4.5 %convolution_convert_fusion.1 = bf16[256,5120]{1,0:T(8,128)(2,1)S(1)} fusion(bf16[512,5120]{0,1:T(8,128)(2,1)} %all-gather.12.cloned.1.call-done, f32[256,512]{1,0:T(8,128)} %copy.46, f32[256,512]{1,0:T(8,128)} %copy.43, f32[512]{0:T(512)S(1)} %copy-done.10, f32[512]{0:T(512)S(1)} %mul.203, bf16[256,1024]{1,0:T(8,128)(2,1)S(1)} %fusion.12), kind=kOutput, calls=%fused_computation.1 | convolution fusion | flops 1345060864 | bytes 9441280 | tf_op jit(solution)/shard_map/dot_general | solution.py:106
  266.0 2.6 copy.50
  269.2 0.2 copy.47
  269.5 0.2 copy.49
  269.9 1.2 fusion.19
  271.0 29.0 %reduce-scatter.4.cloned.1.call-done = bf16[640,256]{1,0:T(8,128)(2,1)} async-done(((bf16[5120,256]{1,0:T(8,128)(2,1)}), bf16[640,256]{1,0:T(8,128)(2,1)}) %reduce-scatter.4.cloned.1.call-update) | async-done | bytes 327696
  300.1 1.9 copy.51
  (56 shorter events, 2.2 us)
Async XLA Ops:
  8.0 2.8 copy-start.9
  8.0 138.8 %all-reduce.3.cloned.1.call-start = ((), (), s32[]{:S(2)}) async-start(), calls=%async_computation.6 | async-start | bytes 8388608
  14.1 2.6 copy-start.8
  14.1 2.8 copy-start.5
  14.1 25.0 %copy-start.11 = (u32[128]{0:T(128)S(1)}, u32[128]{0:T(128)}, u32[]{:S(2)}) copy-start(u32[128]{0:T(128)} %constant.39) | copy-start | bytes 1540
  14.2 136.6 %copy-start.6 = (f32[8]{0:T(128)S(1)}, f32[8]{0:T(128)}, u32[]{:S(2)}) copy-start(f32[8]{0:T(128)} %param.17) | copy-start | bytes 100
  14.2 136.6 %all-gather.6.cloned.1.call-start = ((), (), s32[]{:S(2)}) async-start(), calls=%async_computation.1 | async-start | bytes 2949120 | tf_op jit(solution)/shard_map/all_gather | solution.py:77
  14.8 139.9 %all-gather.10.cloned.1.call-start = ((), (), s32[]{:S(2)}) async-start(), calls=%async_computation.3 | async-start | bytes 5570560 | tf_op jit(solution)/shard_map/all_gather | solution.py:81
  15.3 187.8 %all-gather.8.cloned.1.call-start = ((), (), s32[]{:S(2)}) async-start(), calls=%async_computation.2 | async-start | bytes 11141120 | tf_op jit(solution)/shard_map/all_gather | solution.py:80
  15.9 137.6 %copy-start.7 = (f32[8]{0:T(128)S(1)}, f32[8]{0:T(128)}, u32[]{:S(2)}) copy-start(f32[8]{0:T(128)} %param.18) | copy-start | bytes 100
  15.9 245.6 %all-gather.12.cloned.1.call-start = ((), (), s32[]{:S(2)}) async-start(), calls=%async_computation.4 | async-start | bytes 5570560 | tf_op jit(solution)/shard_map/all_gather | solution.py:108
  16.7 283.4 %reduce-scatter.4.cloned.1.call-start = ((), (), s32[]{:S(2)}) async-start(), calls=%async_computation.5 | async-start | bytes 2949120
  150.8 3.9 %copy-start = (bf16[1,256,5120]{2,1,0:T(8,128)(2,1)S(1)}, bf16[1,256,5120]{2,1,0:T(8,128)(2,1)}, u32[]{:S(2)}) copy-start(bf16[1,256,5120]{2,1,0:T(8,128)(2,1)} %all-gather.6.cloned.1.call-done) | copy-start | bytes 7864324
  158.6 1.1 copy-start.1
  221.6 1.0 copy-start.3
  221.6 1.1 copy-start.4
  225.2 36.3 %copy-start.10 = (f32[512]{0:T(512)S(1)}, f32[512]{0:T(512)}, u32[]{:S(2)}) copy-start(f32[512]{0:T(512)} %param.20) | copy-start | bytes 6148
  268.9 1.0 copy-start.2
Sparse Core Ops, SparseCore 0:
  14.3 132.4 all-reduce.2
Sparse Core Ops, SparseCore 1:
  16.3 30.0 all-gather.5
  48.4 60.9 all-gather.9
  111.4 91.7 all-gather.7
  205.4 56.1 all-gather.11
  268.7 31.4 reduce-scatter.3
where the time goes:
time: 312 us; the launch traced here: 310 us
  waiting for transfers between devices  215 us (69%)
  local copies, waits for them, and re-layouts  27.6 us (9%)
  matrix products  27.1 us (9%)
  blocking collectives  22.1 us (7%)
  between operations  16 us (5%)
    unnamed x8, waiting for transfers between devices  138 us
    all_gather x1, waiting for transfers between devices, shards(): lax.all_gather(w_zx, 'pool', axis=0, tiled=True)  42.6 us
    all_gather x1, waiting for transfers between devices, shards(): lax.all_gather(w_out, 'pool', axis=1, tiled=True)  34.2 us
    unnamed x31, local copies, waits for them, and re-layouts  23.9 us
    all_gather x1, blocking collectives, shards(): lax.all_gather(w_dt, 'pool', axis=0, tiled=True)  22.1 us
    dot_general x3, matrix products, shards(): jnp.dot(flat, piece.reshape(count, -1), preferred_element_type=jnp.float32)  13.7 us
  transfers between devices with their start and end apart: 6, of which 4 were waited for; matrix products, arithmetic and copies ran while one was open for 13% of the time, Pallas kernels for 0%

commit v1 on v0

v1 whole, which is shorter than its diff:
```python
import jax
import jax.numpy as jnp
from jax import lax
from jax.experimental import pallas as pl
from jax.experimental.pallas import tpu as pltpu
from jax.sharding import PartitionSpec as P

F32 = jnp.float32
BF16 = jnp.bfloat16
MESH = pl.DeviceIdType.MESH
VMEM = pltpu.VMEM

HEADS_HERE = 8
N_SEM = 176
CH = 384


def dot_nn(a, b):
    return lax.dot_general(a, b, (((1,), (0,)), ((), ())), preferred_element_type=F32)


def dot_nt(a, b):
    return lax.dot_general(a, b, (((1,), (1,)), ((), ())), preferred_element_type=F32)


def dot_tn(a, b):
    return lax.dot_general(a, b, (((0,), (0,)), ((), ())), preferred_element_type=F32)


def body(
    snap,
    hid,
    wcat,
    wout_t,
    pool,
    small,
    mix_out,
    fin_out,
    xs_,
    ws_,
    p2,
    p1,
    p3,
    r2a,
    r2b,
    r1a,
    r1b,
    pz,
    maps,
    f2,
    f1,
    f3,
    tt,
    q2a,
    q2b,
    q1a,
    q1b,
    g1,
    g3,
    v2a,
    v2b,
    v1a,
    v1b,
    start,
    nb,
    wo,
    keep,
    cs,
    cr,
    o2,
    o1,
    o3,
    e2a,
    e2b,
    e1a,
    e1b,
    fs,
    mt,
    ss,
    rs,
):
    p = lax.axis_index("pool")
    h = lax.axis_index("head")
    y = p // 4
    z = lax.rem(p, 4)
    x = h // 2
    c = lax.rem(h, 2)
    sz = lax.rem(z, 2)
    zc = z // 2

    def m4(v):
        return lax.rem(v, 4)

    def dev(yy, zz, xx, cc):
        return (yy * 4 + zz, xx * 2 + cc)

    yp, ym = dev(m4(y + 1), z, x, c), dev(m4(y + 3), z, x, c)
    zp, zm = dev(y, m4(z + 1), x, c), dev(y, m4(z + 3), x, c)
    xp, xm = dev(y, z, m4(x + 1), c), dev(y, z, m4(x + 3), c)
    sib = dev(y, z, x, 1 - c)

    used = [0]
    sent = []

    def take(n=1):
        i = used[0]
        used[0] += n
        assert used[0] <= N_SEM
        return i

    def copy_of(src, dst, to, si, ri):
        return pltpu.make_async_remote_copy(
            src_ref=src, dst_ref=dst, send_sem=ss.at[si], recv_sem=rs.at[ri], device_id=to, device_id_type=MESH
        )

    def send(src, dst, to):
        i = take()
        cp = copy_of(src, dst, to, i, i)
        cp.start()
        sent.append(cp)
        return cp

    def mo(v, n):
        return pl.multiple_of(v, n)

    barrier = pltpu.get_barrier_semaphore()
    peers = [(p, lax.rem(h + i, 8)) for i in range(1, 8)]
    peers += [dev(y, m4(z + i), x, cc) for i in range(1, 4) for cc in range(2)]
    peers += [yp, ym]
    for peer in peers:
        pl.semaphore_signal(barrier, inc=1, device_id=peer, device_id_type=MESH)
    pl.semaphore_wait(barrier, len(peers))

    hs_sem = take(4)
    hr_sem = take(4)
    h0_local = []

    def x_block(req, half_off, rows, xx):
        return xs_.at[pl.ds(mo(req * 256 + half_off, 64), rows), pl.ds(mo(xx * 384, 128), 384)]

    def h0():
        for s in range(2):
            for d in range(2):
                local = (z == 2 * c + s) & (c == d)
                src = hid.at[pl.ds(d * 128, 128), pl.ds(256 * s, 384)]
                dst = x_block(z, d * 128, 128, x)
                cp = copy_of(src, dst, dev(y, 2 * c + s, x, d), hs_sem + 2 * s + d, hr_sem + z)
                h0_local.append((local, cp))

                @pl.when(jnp.logical_not(local))
                def _(cp=cp):
                    cp.start()

                @pl.when(local)
                def _(s=s, d=d):
                    xs_[pl.ds(mo(z * 256 + d * 128, 64), 128), pl.ds(mo(x * 384, 128), 384)] = hid[
                        d * 128 : d * 128 + 128, 256 * s : 256 * s + 384
                    ]

    hc = {}

    def hs(rr):
        zr = m4(z + rr)
        blk = x_block(zr, c * 128, 128, x)
        got = copy_of(blk, blk, sib, hs_sem, hr_sem + zr)
        if rr == 0:

            @pl.when(c != zc)
            def _():
                got.wait_recv()
        else:
            got.wait_recv()
        hc[rr, "p"] = send(blk, blk, xp)
        hc[rr, "m"] = send(blk, blk, xm)
        hc[rr, "s0"] = send(blk, blk, sib)

    def hf(rr):
        zr = m4(z + rr)
        hc[rr, "p"].wait_recv()
        fw = x_block(zr, c * 128, 64, m4(x + 3))
        hc[rr, "fp"] = send(fw, fw, xp)
        blk = x_block(zr, c * 128, 128, m4(x + 3))
        hc[rr, "s1"] = send(blk, blk, sib)
        hc[rr, "m"].wait_recv()
        fw = x_block(zr, c * 128 + 64, 64, m4(x + 1))
        hc[rr, "fm"] = send(fw, fw, xm)
        blk = x_block(zr, c * 128, 128, m4(x + 1))
        hc[rr, "s2"] = send(blk, blk, sib)

    def hg(rr):
        zr = m4(z + rr)
        hc[rr, "fp"].wait_recv()
        hc[rr, "fm"].wait_recv()
        blk = x_block(zr, c * 128, 128, m4(x + 2))
        hc[rr, "s3"] = send(blk, blk, sib)

    def hw(rr):
        for k in ("s0", "s1", "s2", "s3"):
            hc[rr, k].wait_recv()

    def w_block(i, off, rows, n):
        return ws_.at[pl.ds(mo(384 * i + 64 * sz + off, 32), rows), pl.ds(n * CH, CH)]

    wc = {}

    def w_init():
        for i in range(4):
            ws_[pl.ds(mo(384 * i + 320 * (1 - sz), 64), 64), :] = jnp.zeros((64, 3 * CH), BF16)
        ws_[pl.ds(mo(384 * y + 64 * sz, 64), 320), :] = wcat[...]

    def w0(n):
        src = wcat.at[:, pl.ds(n * CH, CH)]
        dst = w_block(y, 0, 320, n)
        wc[n, "p"] = send(src, dst, yp)
        wc[n, "m"] = send(src, dst, ym)

    def wf(n):
        wc[n, "p"].wait_recv()
        fw = w_block(m4(y + 3), 0, 160, n)
        wc[n, "fp"] = send(fw, fw, yp)
        wc[n, "m"].wait_recv()
        fw = w_block(m4(y + 1), 160, 160, n)
        wc[n, "fm"] = send(fw, fw, ym)

    def wg(n):
        wc[n, "fp"].wait_recv()
        wc[n, "fm"].wait_recv()

    pc = {}

    def part(n, rr):
        zr = m4(z + rr)
        return dot_nn(xs_[pl.ds(mo(zr * 256, 256), 256), :], ws_[:, n * CH : (n + 1) * CH])

    def pa(n):
        p2[n] = part(n, 2).astype(BF16)
        pc[n, "2a"] = send(p2.at[n, pl.ds(0, 128)], r2a.at[n], zp)
        pc[n, "2b"] = send(p2.at[n, pl.ds(128, 128)], r2b.at[n], zm)

    def pb(n):
        a = part(n, 1)
        p1[n, 128:] = a[128:].astype(BF16)
        pc[n, "1ah"] = send(p1.at[n, pl.ds(128, 128)], r1a.at[n, pl.ds(128, 128)], zp)
        b = part(n, 3)
        p3[n, :128] = b[:128].astype(BF16)
        pc[n, "1bl"] = send(p3.at[n, pl.ds(0, 128)], r1b.at[n, pl.ds(0, 128)], zm)
        pc[n, "2a"].wait_recv()
        p1[n, :128] = (a[:128] + r2a[n].astype(F32)).astype(BF16)
        pc[n, "1al"] = send(p1.at[n, pl.ds(0, 128)], r1a.at[n, pl.ds(0, 128)], zp)
        pc[n, "2b"].wait_recv()
        p3[n, 128:] = (b[128:] + r2b[n].astype(F32)).astype(BF16)
        pc[n, "1bh"] = send(p3.at[n, pl.ds(128, 128)], r1b.at[n, pl.ds(128, 128)], zm)

    def pd(n):
        own = part(n, 0)
        for k in ("1ah", "1al", "1bl", "1bh"):
            pc[n, k].wait_recv()
        pz[:, n * CH : (n + 1) * CH] = (own + r1a[n].astype(F32) + r1b[n].astype(F32)).astype(BF16)

    mr_sem = take(8)
    mc = []

    def m0():
        maps[h] = pz[:, :128]
        for i in range(1, 8):
            si = take()
            cp = copy_of(pz.at[:, pl.ds(0, 128)], maps.at[h], (p, lax.rem(h + i, 8)), si, mr_sem + h)
            cp.start()
            sent.append(cp)

    def mw():
        for i in range(1, 8):
            o = lax.rem(h + i, 8)
            copy_of(maps.at[o], maps.at[o], sib, mr_sem, mr_sem + o).wait_recv()

    sc = {}
    axes = (((y, yp, ym), (z, zp, zm)), ((z, zp, zm), (y, yp, ym)))

    def pick(half, a, b):
        r = a * 4 + b if half == 0 else b * 4 + a
        idx = snap[r]
        v = pool[lax.rem(idx, 8), half * 256 : half * 256 + 256, :]
        return jnp.where(idx // 8 == p, v, jnp.zeros_like(v))

    def s0(u):
        (a, ap, am), _ = axes[u]
        for b in range(4):
            f2[u, b] = pick(u, m4(a + 2), b)
            if b == 1:
                sc[u, "2a"] = send(f2.at[u, pl.ds(0, 2)], q2a.at[u], ap)
        sc[u, "2b"] = send(f2.at[u, pl.ds(2, 2)], q2b.at[u], am)
        for b in (2, 3):
            f1[u, b] = pick(u, m4(a + 1), b)
        sc[u, "1ah"] = send(f1.at[u, pl.ds(2, 2)], q1a.at[u, pl.ds(2, 2)], ap)
        for b in (0, 1):
            f3[u, b] = pick(u, m4(a + 3), b)
        sc[u, "1bl"] = send(f3.at[u, pl.ds(0, 2)], q1b.at[u, pl.ds(0, 2)], am)

    def s1(u):
        (a, ap, am), _ = axes[u]
        sc[u, "2a"].wait_recv()
        for b in (0, 1):
            f1[u, b] = pick(u, m4(a + 1), b) + q2a[u, b]
        sc[u, "1al"] = send(f1.at[u, pl.ds(0, 2)], q1a.at[u, pl.ds(0, 2)], ap)
        sc[u, "2b"].wait_recv()
        for b in (2, 3):
            f3[u, b] = pick(u, m4(a + 3), b) + q2b[u, b - 2]
        sc[u, "1bh"] = send(f3.at[u, pl.ds(2, 2)], q1b.at[u, pl.ds(2, 2)], am)

    def s2(u):
        (a, _, _), (b0, bp, bm) = axes[u]
        sc[u, "1ah"].wait_recv()
        sc[u, "1bl"].wait_recv()
        sc[u, "1al"].wait_recv()
        sc[u, "1bh"].wait_recv()
        for b in range(4):
            tt[u, b] = pick(u, a, b) + q1a[u, b] + q1b[u, b]
        far, nxt, prv = m4(b0 + 2), m4(b0 + 1), m4(b0 + 3)
        sc[u, "v2a"] = send(tt.at[u, far, pl.ds(0, 128)], v2a.at[u], bp)
        sc[u, "v2b"] = send(tt.at[u, far, pl.ds(128, 128)], v2b.at[u], bm)
        sc[u, "v1ah"] = send(tt.at[u, nxt, pl.ds(128, 128)], v1a.at[u, pl.ds(128, 128)], bp)
        sc[u, "v1bl"] = send(tt.at[u, prv, pl.ds(0, 128)], v1b.at[u, pl.ds(0, 128)], bm)

    def s3(u):
        _, (b0, bp, bm) = axes[u]
        nxt, prv = m4(b0 + 1), m4(b0 + 3)
        sc[u, "v2a"].wait_recv()
        g1[u] = tt[u, nxt, :128, :] + v2a[u]
        sc[u, "v1al"] = send(g1.at[u], v1a.at[u, pl.ds(0, 128)], bp)
        sc[u, "v2b"].wait_recv()
        g3[u] = tt[u, prv, 128:, :] + v2b[u]
        sc[u, "v1bh"] = send(g3.at[u], v1b.at[u, pl.ds(128, 128)], bm)

    def s4(u):
        _, (b0, _, _) = axes[u]
        for k in ("v1ah", "v1bl", "v1al", "v1bh"):
            sc[u, k].wait_recv()
        start[u * 256 : u * 256 + 256] = tt[u, b0] + v1a[u] + v1b[u]

    oc = {}

    def wo0():
        wo[y] = wout_t[...]
        oc["p"] = send(wout_t, wo.at[y], yp)
        oc["m"] = send(wout_t, wo.at[y], ym)

    def wof():
        oc["p"].wait_recv()
        fw = wo.at[m4(y + 3), pl.ds(0, 160)]
        oc["fp"] = send(fw, fw, yp)
        oc["m"].wait_recv()
        fw = wo.at[m4(y + 1), pl.ds(160, 160)]
        oc["fm"] = send(fw, fw, ym)

    def wog():
        oc["fp"].wait_recv()
        oc["fm"].wait_recv()

    nc = {}

    def scan():
        dtile = pz[:, :128].astype(F32)
        dtile = jnp.where(c == 0, pltpu.roll(dtile, 64, 1), dtile)
        v = dtile + small[0:1, :128]
        dt = jnp.maximum(v, 0.0) + jnp.log1p(jnp.exp(-jnp.abs(v)))
        rowi = lax.broadcasted_iota(jnp.int32, (256, 256), 0)
        coli = lax.broadcasted_iota(jnp.int32, (256, 256), 1)
        lower = rowi >= coli
        tri = jnp.where(lower, 1.0, 0.0).astype(F32)
        cum = lax.dot_general(
            tri,
            -(small[1:2, :128] * dt),
            (((1,), (0,)), ((), ())),
            precision=lax.Precision.HIGHEST,
            preferred_element_type=F32,
        )
        ecum = jnp.exp(cum)
        tail = jnp.exp(cum[255:256, :] - cum) * dt
        cum_t = cum.T
        dt_t = dt.T
        lane = lax.broadcasted_iota(jnp.int32, (256, 128), 1)
        first = lane < 64
        bmat = jnp.concatenate([jnp.where(first, maps[2 * i], maps[2 * i + 1]) for i in range(2)], axis=1)
        cmat = jnp.concatenate([jnp.where(first, maps[4 + 2 * i], maps[5 + 2 * i]) for i in range(2)], axis=1)
        scores = dot_nt(cmat, bmat)
        r128 = lax.broadcasted_iota(jnp.int32, (128, 128), 0) // 64
        c128 = lax.broadcasted_iota(jnp.int32, (128, 128), 1) // 64
        same = jnp.where(r128 == c128, 1.0 / 64.0, 0.0).astype(BF16)
        rows_first = lax.broadcasted_iota(jnp.int32, (128, 256), 0) < 64
        for k in range(4):
            lo, hi = 2 * k, 2 * k + 1
            cols = slice(128 * k, 128 * k + 128)
            xv = pz[:, 640 + 128 * k : 768 + 128 * k]
            gate = pz[:, 128 + 128 * k : 256 + 128 * k].astype(F32)
            xf = xv.astype(F32)

            def within(q):
                spread = jnp.where(lower, cum[:, q : q + 1] - cum_t[q : q + 1, :], -1e30)
                mix = jnp.exp(spread) * dt_t[q : q + 1, :] * scores
                return dot_nn(mix.astype(BF16), xv)

            def spread2(a):
                return jnp.where(first, a[:, lo : lo + 1], a[:, hi : hi + 1])

            s_in = start[128 * k : 128 * k + 128, :]
            carried = spread2(ecum) * dot_nt(cmat, s_in)
            scanned = jnp.where(first, within(lo), within(hi)) + carried
            gated = (scanned + small[2:3, cols] * xf) * (gate / (1.0 + jnp.exp(-gate)))
            sq = gated * gated
            sq_hi = sq.astype(BF16)
            sq_lo = (sq - sq_hi.astype(F32)).astype(BF16)
            meansq = dot_nn(sq_hi, same) + dot_nn(sq_lo, same)
            normed = gated * lax.rsqrt(meansq + 1e-05) * small[3:4, cols]
            nb[z, :, cols] = normed.astype(BF16)
            blk = nb.at[z, :, pl.ds(128 * k, 128)]
            nc[k, "p"] = send(blk, blk, zp)
            nc[k, "m"] = send(blk, blk, zm)
            weighted = (xf * spread2(tail)).astype(BF16)
            last = jnp.where(rows_first, ecum[255:256, lo : lo + 1], ecum[255:256, hi : hi + 1])
            fin_out[128 * k : 128 * k + 128, :] = last * s_in.astype(F32) + dot_tn(weighted, bmat)

    def nf():
        for k in range(4):
            nc[k, "p"].wait_recv()
            fw = nb.at[m4(z + 3), pl.ds(0, 128), pl.ds(128 * k, 128)]
            nc[k, "fp"] = send(fw, fw, zp)
            nc[k, "m"].wait_recv()
            fw = nb.at[m4(z + 1), pl.ds(128, 128), pl.ds(128 * k, 128)]
            nc[k, "fm"] = send(fw, fw, zm)

    def ng():
        for k in range(4):
            nc[k, "fp"].wait_recv()
            nc[k, "fm"].wait_recv()

    xc = {}
    fr_sem = take(4)
    fin_copies = []

    def oa(rr):
        n = nb[m4(z + rr)]
        for ii in (2, 1, 3, 0):
            o = dot_nt(wo[m4(x + ii)], n)
            left, right = o[:, :128], o[:, 128:]
            keep[rr, ii] = jnp.where(c == 0, left, right)
            cs[rr, ii] = jnp.where(c == 0, right, left).astype(BF16)
        xc[rr, "c"] = send(cs.at[rr], cr.at[rr], sib)

    def ob(rr):
        xc[rr, "c"].wait_recv()
        o2[rr] = (keep[rr, 2] + cr[rr, 2].astype(F32)).astype(BF16)
        xc[rr, "2a"] = send(o2.at[rr, pl.ds(0, 160)], e2a.at[rr], xp)
        xc[rr, "2b"] = send(o2.at[rr, pl.ds(160, 160)], e2b.at[rr], xm)
        o1[rr, 160:] = (keep[rr, 1, 160:] + cr[rr, 1, 160:].astype(F32)).astype(BF16)
        xc[rr, "1ah"] = send(o1.at[rr, pl.ds(160, 160)], e1a.at[rr, pl.ds(160, 160)], xp)
        o3[rr, :160] = (keep[rr, 3, :160] + cr[rr, 3, :160].astype(F32)).astype(BF16)
        xc[rr, "1bl"] = send(o3.at[rr, pl.ds(0, 160)], e1b.at[rr, pl.ds(0, 160)], xm)

    def od(rr):
        xc[rr, "2a"].wait_recv()
        o1[rr, :160] = (keep[rr, 1, :160] + cr[rr, 1, :160].astype(F32) + e2a[rr].astype(F32)).astype(BF16)
        xc[rr, "1al"] = send(o1.at[rr, pl.ds(0, 160)], e1a.at[rr, pl.ds(0, 160)], xp)
        xc[rr, "2b"].wait_recv()
        o3[rr, 160:] = (keep[rr, 3, 160:] + cr[rr, 3, 160:].astype(F32) + e2b[rr].astype(F32)).astype(BF16)
        xc[rr, "1bh"] = send(o3.at[rr, pl.ds(160, 160)], e1b.at[rr, pl.ds(160, 160)], xm)

    def oe(rr):
        for k in ("1ah", "1bl", "1al", "1bh"):
            xc[rr, k].wait_recv()
        total = keep[rr, 0] + cr[rr, 0].astype(F32) + e1a[rr].astype(F32) + e1b[rr].astype(F32)
        fs[rr] = total.astype(BF16)
        dst = mt.at[pl.ds(mo(sz * 320, 64), 320), pl.ds(mo(c * 128, 128), 128)]
        cp = copy_of(fs.at[rr], dst, dev(y, m4(z + rr), x, zc), take(), fr_sem + 2 * sz + c)
        if rr == 0:

            @pl.when(c != zc)
            def _():
                cp.start()

            @pl.when(c == zc)
            def _():
                mt[pl.ds(mo(sz * 320, 64), 320), pl.ds(mo(c * 128, 128), 128)] = fs[0]
        else:
            cp.start()
        fin_copies.append((rr, cp))

    def of():
        for s in range(2):
            for cc in range(2):
                dst = mt.at[pl.ds(s * 320, 320), pl.ds(cc * 128, 128)]
                got = copy_of(dst, dst, sib, hs_sem, fr_sem + 2 * s + cc)
                local = (z == 2 * c + s) & (c == cc)

                @pl.when(jnp.logical_not(local))
                def _(got=got):
                    got.wait_recv()

        mix_out[...] = mt[...]

    h0()
    w0(0)
    s0(1)
    w_init()
    hs(2)
    hs(1)
    hs(3)
    hs(0)
    hf(2)
    hf(1)
    wf(0)
    w0(1)
    hf(3)
    hg(2)
    hf(0)
    hg(1)
    hg(3)
    hg(0)
    wg(0)
    hw(2)
    pa(0)
    hw(1)
    hw(3)
    s1(1)
    pb(0)
    wf(1)
    w0(2)
    hw(0)
    wg(1)
    pa(1)
    pd(0)
    m0()
    wf(2)
    s0(0)
    pb(1)
    wg(2)
    pa(2)
    s2(1)
    pd(1)
    pb(2)
    s3(1)
    s1(0)
    pd(2)
    s4(1)
    wo0()
    s2(0)
    s3(0)
    wof()
    s4(0)
    mw()
    scan()
    wog()
    oa(0)
    nf()
    ob(0)
    oa(1)
    od(0)
    ob(1)
    oa(3)
    od(1)
    ob(3)
    oe(0)
    ng()
    oa(2)
    od(3)
    ob(2)
    oe(1)
    oe(3)
    od(2)
    oe(2)
    of()

    for cp in sent:
        cp.wait_send()
    for local, cp in h0_local:

        @pl.when(jnp.logical_not(local))
        def _(cp=cp):
            cp.wait_send()

    for rr, cp in fin_copies:
        if rr == 0:

            @pl.when(c != zc)
            def _(cp=cp):
                cp.wait_send()
        else:
            cp.wait_send()


def shards(hidden, snap_map, pool_states, w_zx, w_bc, w_dt, dt_bias, decay_rate, skip, norm_gain, w_out):
    h = lax.axis_index("head")
    c = lax.rem(h, 2)
    w_b = lax.dynamic_slice_in_dim(w_bc, h * 64, 64, axis=1)
    w_d = jnp.pad(w_dt, ((0, 0), (0, 56)))
    tile = jnp.where(c == 0, jnp.concatenate([w_b, w_d], 1), jnp.concatenate([w_d, w_b], 1))
    wcat = jnp.concatenate([tile, w_zx.reshape(320, 1024)], axis=1)
    small = jnp.stack(
        [
            jnp.pad(dt_bias, (0, 504)),
            jnp.pad(decay_rate, (0, 504)),
            jnp.repeat(skip, 64),
            norm_gain,
        ]
        + [jnp.zeros((512,), F32)] * 4
    )
    vm = pl.BlockSpec(memory_space=VMEM)
    scratch = [
        VMEM((1024, 1536), BF16),
        VMEM((1536, 3 * CH), BF16),
        *[VMEM((3, 256, CH), BF16)] * 3,
        *[VMEM((3, 128, CH), BF16)] * 2,
        *[VMEM((3, 256, CH), BF16)] * 2,
        VMEM((256, 3 * CH), BF16),
        VMEM((8, 256, 128), BF16),
        *[VMEM((2, 4, 256, 256), BF16)] * 4,
        *[VMEM((2, 2, 256, 256), BF16)] * 2,
        *[VMEM((2, 4, 256, 256), BF16)] * 2,
        *[VMEM((2, 128, 256), BF16)] * 4,
        *[VMEM((2, 256, 256), BF16)] * 2,
        VMEM((512, 256), BF16),
        VMEM((4, 256, 512), BF16),
        VMEM((4, 320, 512), BF16),
        VMEM((4, 4, 320, 128), F32),
        *[VMEM((4, 4, 320, 128), BF16)] * 2,
        *[VMEM((4, 320, 128), BF16)] * 3,
        *[VMEM((4, 160, 128), BF16)] * 2,
        *[VMEM((4, 320, 128), BF16)] * 3,
        VMEM((640, 256), BF16),
        pltpu.SemaphoreType.DMA((N_SEM,)),
        pltpu.SemaphoreType.DMA((N_SEM,)),
    ]
    mixed_t, final = pl.pallas_call(
        body,
        out_shape=(jax.ShapeDtypeStruct((640, 256), BF16), jax.ShapeDtypeStruct((512, 256), F32)),
        in_specs=[pl.BlockSpec(memory_space=pltpu.SMEM)] + [vm] * 5,
        out_specs=(vm, vm),
        scratch_shapes=scratch,
        compiler_params=pltpu.CompilerParams(
            collective_id=0, has_side_effects=True, vmem_limit_bytes=56 * 1024 * 1024
        ),
    )(snap_map, hidden.reshape(256, 640), wcat, w_out.T, pool_states.reshape(8, 512, 256), small)
    return mixed_t.T.reshape(1, 256, 640), final.reshape(1, 8, 64, 256)


def solution(mesh):
    in_specs = (
        P("pool", None, "head"),
        P(),
        P("pool", "head", None, None),
        P("pool", None, "head"),
        P("pool", None),
        P("pool", "head"),
        P("head"),
        P("head"),
        P("head"),
        P("head"),
        P("head", "pool"),
    )
    out_specs = (P("pool", None, "head"), P("pool", "head", None, None))
    return jax.shard_map(shards, mesh=mesh, in_specs=in_specs, out_specs=out_specs, check_vma=False)
```

time: 312 us -> 129 us (0.41)
  waiting for transfers between devices: 215 us -> 0 us
  Pallas kernels: 0 us -> 117 us
  matrix products: 27.1 us -> 0 us
  blocking collectives: 22.1 us -> 0 us
  local copies, waits for them, and re-layouts: 27.6 us -> 9.34 us
  between operations: 16 us -> 0.68 us
    unnamed x8 -> x0, waiting for transfers between devices: 138 us -> none
    pallas_call x0 -> x1, Pallas kernels: none -> 117 us  [shards(): pl.pallas_call(body, out_shape=(jax.ShapeDtypeStruct((640, 256), BF16), j...]
    all_gather x4 -> x0, waiting for transfers between devices: 76.8 us -> none  [the longest x1 42.6 us: shards(): lax.all_gather(w_zx, 'pool', axis=0, tiled=True)]
    dot_general x9 -> x0, matrix products: 27.1 us -> none  [the longest x3 13.7 us: shards(): jnp.dot(flat, piece.reshape(count, -1), preferred_element_type=jnp.float32)]
    all_gather x1 -> x0, blocking collectives: 22.1 us -> none  [shards(): lax.all_gather(w_dt, 'pool', axis=0, tiled=True)]
    unnamed x31 -> x6, local copies, waits for them, and re-layouts: 23.9 us -> 5.75 us
  transfers between devices with their start and end apart: 6 -> 0, of which waited for: 4 -> 0; matrix products, arithmetic and copies ran while one was open for 13% -> 0% of each run, Pallas kernels for 0% -> 0%
where the time goes in v1:
time: 129 us; the launch traced here: 128 us
  Pallas kernels  117 us (91%)
  local copies, waits for them, and re-layouts  9.34 us (7%)
    pallas_call x1, Pallas kernels, shards(): pl.pallas_call(body, out_shape=(jax.ShapeDtypeStruct((640, 256), BF16), j...  117 us
    unnamed x6, local copies, waits for them, and re-layouts  5.75 us

profile of v1, /device:TPU:1, one launch (start us, length us, event | category | flops | bytes accessed | tf_op | source)
XLA Modules:
  0.0 128.4 jit_solution(14966509659951815916)
XLA Ops:
  0.6 0.0 copy-start
  0.7 0.7 pad.12
  1.4 0.7 pad.13
  2.0 0.7 broadcast_in_dim.3
  2.7 0.1 stack_reshape.3
  2.8 1.3 %stack.19.small = f32[8,512]{1,0:T(8,128)} concatenate(f32[1,512]{1,0:T(1,128)S(1)} %bitcast.19, f32[1,512]{1,0:T(1,128)S(1)} %bitcast.20, f32[1,512]{1,0:T(1,128)S(1)} %stack_reshape.3, f32[1,512]{1,0:T(1,128)} %bitcast.21, f32[4,512]{1,0:T(4,128)S(1)} %stack.18), dimensions={0} | concatenate | bytes 32768 | tf_op jit(solution)/shard_map/stack | solution.py:597
  4.1 0.0 copy-done
  4.1 0.1 constant_dynamic-slice_fusion
  4.2 0.8 copy.13
  5.1 0.1 maximum_select_fusion
  5.2 1.2 copy.15
  6.4 0.9 pad_maximum_fusion.wcat
  7.3 117.3 %shard_map.122 = (bf16[640,256]{1,0:T(8,128)(2,1)}, f32[512,256]{1,0:T(8,128)}) custom-call(s32[16]{0:T(128)} %snap.1, bf16[256,640]{1,0:T(8,128)(2,1)} %bitcast.16, bf16[320,1152]{1,0:T(8,128)(2,1)} %pad_maximum_fusion.wcat, bf16[320,512]{1,0:T(8,128)(2,1)} %bitcast.17, bf16[8,512,256]{2,1,0:T(8,128)(2,1)} %bitcast.13, f32[8,512]{1,0:T(8,128)} %stack.19.small), custom_call_target="tpu_custom_call" | custom-call | tf_op jit(solution)/shard_map/pallas_call | solution.py:632
  124.7 1.9 %copy.14 = bf16[1,256,640]{2,1,0:T(8,128)(2,1)} copy(bf16[1,256,640]{1,2,0:T(8,128)(2,1)} %bitcast.18) | data formatting | bytes 655360
  126.6 1.9 %copy.17 = f32[1,8,64,256]{3,2,1,0:T(8,128)} copy(f32[1,8,64,256]{3,2,1,0:T(8,128)} %bitcast.15) | data formatting | bytes 1048576
  (2 shorter events, 0.0 us)
Async XLA Ops:
  0.6 3.5 %copy-start = (bf16[320,512]{1,0:T(8,128)(2,1)S(1)}, bf16[320,512]{1,0:T(8,128)(2,1)}, u32[]{:S(2)}) copy-start(bf16[320,512]{1,0:T(8,128)(2,1)} %param.15) | copy-start | bytes 983044

commit v2 on v1

--- a/solution.py
+++ b/solution.py
@@ -10,11 +10,107 @@
 MESH = pl.DeviceIdType.MESH
 VMEM = pltpu.VMEM
 
-HEADS_HERE = 8
 N_SEM = 176
 CH = 384
 
 
+ORDER = (
+    "h0",
+    "w_cat",
+    "w0 0",
+    "s0 1",
+    "w0 1",
+    "w0 2",
+    "w_init",
+    "s0 0",
+    "hs 2",
+    "hs 1",
+    "hs 3",
+    "hs 0",
+    "hf 2",
+    "hf 1",
+    "wf 0",
+    "hf 3",
+    "hg 2",
+    "hf 0",
+    "hg 1",
+    "hg 3",
+    "hg 0",
+    "s1 1",
+    "wf 1",
+    "wg 0",
+    "hw 2",
+    "pa 0",
+    "hw 1",
+    "hw 3",
+    "pb 0",
+    "wf 2",
+    "hw 0",
+    "wg 1",
+    "pa 1",
+    "pd 0",
+    "m0",
+    "s1 0",
+    "pb 1",
+    "wg 2",
+    "pa 2",
+    "s2 1",
+    "pd 1",
+    "pb 2",
+    "s3 1",
+    "s2 0",
+    "pd 2",
+    "mw",
+    "wo0",
+    "scan_a",
+    "s4 1",
+    "s3 0",
+    "wof",
+    "s4 0",
+    "scan_b 0",
+    "scan_b 1",
+    "scan_b 2",
+    "scan_b 3",
+    "wog",
+    "nw",
+    "wow",
+    "oa 0",
+    "nf 0",
+    "nf 1",
+    "od 0",
+    "oa 1",
+    "oa 3",
+    "ng",
+    "oe 0",
+    "oa 2",
+    "od 1",
+    "od 3",
+    "od 2",
+    "oe 1",
+    "oe 3",
+    "oe 2",
+    "final",
+    "of",
+)
+
+
+class Sent:
+    def __init__(self, copy):
+        self.copy = copy
+        self.got = False
+        copy.start()
+
+    def wait_recv(self):
+        assert not self.got
+        self.got = True
+        self.copy.wait_recv()
+
+    def finish(self):
+        if not self.got:
+            self.wait_recv()
+        self.copy.wait_send()
+
+
 def dot_nn(a, b):
     return lax.dot_general(a, b, (((1,), (0,)), ((), ())), preferred_element_type=F32)
 
@@ -29,13 +125,19 @@
 
 def body(
     snap,
+    bias,
+    rate,
+    skip,
+    gain,
     hid,
-    wcat,
+    wzx,
+    wbc,
+    wdt,
     wout_t,
     pool,
-    small,
     mix_out,
     fin_out,
+    wcat,
     xs_,
     ws_,
     p2,
@@ -62,11 +164,15 @@
     v1a,
     v1b,
     start,
-    nb,
+    wi,
+    wt,
+    bc,
+    ns,
+    nbuf,
     wo,
-    keep,
-    cs,
-    cr,
+    k0,
+    k1,
+    k3,
     o2,
     o1,
     o3,
@@ -115,8 +221,7 @@
 
     def send(src, dst, to):
         i = take()
-        cp = copy_of(src, dst, to, i, i)
-        cp.start()
+        cp = Sent(copy_of(src, dst, to, i, i))
         sent.append(cp)
         return cp
 
@@ -202,6 +307,17 @@
         return ws_.at[pl.ds(mo(384 * i + 64 * sz + off, 32), rows), pl.ds(n * CH, CH)]
 
     wc = {}
+
+    def w_cat():
+        lane = lax.broadcasted_iota(jnp.int32, (320, 128), 1)
+        er = lax.broadcasted_iota(jnp.int32, (8, 128), 0)
+        el = lax.broadcasted_iota(jnp.int32, (8, 128), 1)
+        place = jnp.where(el == er + 64 * (1 - c), 1.0, 0.0).astype(BF16)
+        steps_w = dot_tn(wdt[...], place).astype(BF16)
+        maps_w = wbc[:, pl.ds(mo(x * 128, 128), 128)]
+        wcat[:, :128] = jnp.where(lane // 64 == c, maps_w, steps_w)
+        wcat[:, 128:640] = wzx[:, 0, :]
+        wcat[:, 640:] = wzx[:, 1, :]
 
     def w_init():
         for i in range(4):
@@ -258,7 +374,7 @@
         pz[:, n * CH : (n + 1) * CH] = (own + r1a[n].astype(F32) + r1b[n].astype(F32)).astype(BF16)
 
     mr_sem = take(8)
-    mc = []
+    map_copies = []
 
     def m0():
         maps[h] = pz[:, :128]
@@ -266,7 +382,7 @@
             si = take()
             cp = copy_of(pz.at[:, pl.ds(0, 128)], maps.at[h], (p, lax.rem(h + i, 8)), si, mr_sem + h)
             cp.start()
-            sent.append(cp)
+            map_copies.append(cp)
 
     def mw():
         for i in range(1, 8):
@@ -338,30 +454,53 @@
         start[u * 256 : u * 256 + 256] = tt[u, b0] + v1a[u] + v1b[u]
 
     oc = {}
+    half = pl.ds(mo(c * 128, 128), 128)
 
     def wo0():
-        wo[y] = wout_t[...]
-        oc["p"] = send(wout_t, wo.at[y], yp)
-        oc["m"] = send(wout_t, wo.at[y], ym)
+        for k in range(4):
+            wo[y, k, :, half] = wout_t[:, 128 * k : 128 * k + 128]
+        blk = wo.at[y, :, :, half]
+        oc["p"] = send(blk, blk, yp)
+        oc["m"] = send(blk, blk, ym)
+        oc["s0"] = send(blk, blk, sib)
 
     def wof():
         oc["p"].wait_recv()
-        fw = wo.at[m4(y + 3), pl.ds(0, 160)]
+        fw = wo.at[m4(y + 3), :, pl.ds(0, 160), half]
         oc["fp"] = send(fw, fw, yp)
+        blk = wo.at[m4(y + 3), :, :, half]
+        oc["s1"] = send(blk, blk, sib)
         oc["m"].wait_recv()
-        fw = wo.at[m4(y + 1), pl.ds(160, 160)]
+        fw = wo.at[m4(y + 1), :, pl.ds(160, 160), half]
         oc["fm"] = send(fw, fw, ym)
+        blk = wo.at[m4(y + 1), :, :, half]
+        oc["s2"] = send(blk, blk, sib)
 
     def wog():
         oc["fp"].wait_recv()
         oc["fm"].wait_recv()
+        blk = wo.at[m4(y + 2), :, :, half]
+        oc["s3"] = send(blk, blk, sib)
+
+    def wow():
+        for k in ("s0", "s1", "s2", "s3"):
+            oc[k].wait_recv()
 
     nc = {}
-
-    def scan():
+    fa = {}
+
+    def scan_a():
+        lane1 = lax.broadcasted_iota(jnp.int32, (1, 128), 1)
+
+        def row_of(ref):
+            row = jnp.zeros((1, 128), F32)
+            for q in range(8):
+                row = jnp.where(lane1 == q, ref[q], row)
+            return row
+
         dtile = pz[:, :128].astype(F32)
         dtile = jnp.where(c == 0, pltpu.roll(dtile, 64, 1), dtile)
-        v = dtile + small[0:1, :128]
+        v = dtile + row_of(bias)
         dt = jnp.maximum(v, 0.0) + jnp.log1p(jnp.exp(-jnp.abs(v)))
         rowi = lax.broadcasted_iota(jnp.int32, (256, 256), 0)
         coli = lax.broadcasted_iota(jnp.int32, (256, 256), 1)
@@ -369,7 +508,7 @@
         tri = jnp.where(lower, 1.0, 0.0).astype(F32)
         cum = lax.dot_general(
             tri,
-            -(small[1:2, :128] * dt),
+            -(row_of(rate) * dt),
             (((1,), (0,)), ((), ())),
             precision=lax.Precision.HIGHEST,
             preferred_element_type=F32,
@@ -378,96 +517,124 @@
         tail = jnp.exp(cum[255:256, :] - cum) * dt
         cum_t = cum.T
         dt_t = dt.T
-        lane = lax.broadcasted_iota(jnp.int32, (256, 128), 1)
-        first = lane < 64
-        bmat = jnp.concatenate([jnp.where(first, maps[2 * i], maps[2 * i + 1]) for i in range(2)], axis=1)
-        cmat = jnp.concatenate([jnp.where(first, maps[4 + 2 * i], maps[5 + 2 * i]) for i in range(2)], axis=1)
-        scores = dot_nt(cmat, bmat)
-        r128 = lax.broadcasted_iota(jnp.int32, (128, 128), 0) // 64
-        c128 = lax.broadcasted_iota(jnp.int32, (128, 128), 1) // 64
-        same = jnp.where(r128 == c128, 1.0 / 64.0, 0.0).astype(BF16)
-        rows_first = lax.broadcasted_iota(jnp.int32, (128, 256), 0) < 64
+        first = lax.broadcasted_iota(jnp.int32, (256, 128), 1) < 64
+        for i in range(2):
+            bc[0, :, 128 * i : 128 * i + 128] = jnp.where(first, maps[2 * i], maps[2 * i + 1])
+            bc[1, :, 128 * i : 128 * i + 128] = jnp.where(first, maps[4 + 2 * i], maps[5 + 2 * i])
+        scores = dot_nt(bc[1], bc[0])
         for k in range(4):
-            lo, hi = 2 * k, 2 * k + 1
-            cols = slice(128 * k, 128 * k + 128)
             xv = pz[:, 640 + 128 * k : 768 + 128 * k]
-            gate = pz[:, 128 + 128 * k : 256 + 128 * k].astype(F32)
-            xf = xv.astype(F32)
 
             def within(q):
                 spread = jnp.where(lower, cum[:, q : q + 1] - cum_t[q : q + 1, :], -1e30)
                 mix = jnp.exp(spread) * dt_t[q : q + 1, :] * scores
                 return dot_nn(mix.astype(BF16), xv)
 
-            def spread2(a):
-                return jnp.where(first, a[:, lo : lo + 1], a[:, hi : hi + 1])
-
-            s_in = start[128 * k : 128 * k + 128, :]
-            carried = spread2(ecum) * dot_nt(cmat, s_in)
-            scanned = jnp.where(first, within(lo), within(hi)) + carried
-            gated = (scanned + small[2:3, cols] * xf) * (gate / (1.0 + jnp.exp(-gate)))
-            sq = gated * gated
-            sq_hi = sq.astype(BF16)
-            sq_lo = (sq - sq_hi.astype(F32)).astype(BF16)
-            meansq = dot_nn(sq_hi, same) + dot_nn(sq_lo, same)
-            normed = gated * lax.rsqrt(meansq + 1e-05) * small[3:4, cols]
-            nb[z, :, cols] = normed.astype(BF16)
-            blk = nb.at[z, :, pl.ds(128 * k, 128)]
-            nc[k, "p"] = send(blk, blk, zp)
-            nc[k, "m"] = send(blk, blk, zm)
-            weighted = (xf * spread2(tail)).astype(BF16)
+            cols = slice(128 * k, 128 * k + 128)
+            wi[:, cols] = jnp.where(first, within(2 * k), within(2 * k + 1))
+            w = jnp.where(first, tail[:, 2 * k : 2 * k + 1], tail[:, 2 * k + 1 : 2 * k + 2])
+            wt[:, cols] = (xv.astype(F32) * w).astype(BF16)
+        fa["ecum"] = ecum
+
+    def scan_b(k):
+        ecum = fa["ecum"]
+        lo, hi = 2 * k, 2 * k + 1
+        cols = slice(128 * k, 128 * k + 128)
+        first = lax.broadcasted_iota(jnp.int32, (256, 128), 1) < 64
+        r128 = lax.broadcasted_iota(jnp.int32, (128, 128), 0) // 64
+        c128 = lax.broadcasted_iota(jnp.int32, (128, 128), 1) // 64
+        same = jnp.where(r128 == c128, 1.0 / 64.0, 0.0).astype(BF16)
+        xf = pz[:, 640 + 128 * k : 768 + 128 * k].astype(F32)
+        gate = pz[:, 128 + 128 * k : 256 + 128 * k].astype(F32)
+        s_in = start[cols, :]
+        decay = jnp.where(first, ecum[:, lo : lo + 1], ecum[:, hi : hi + 1])
+        scanned = wi[:, cols] + decay * dot_nt(bc[1], s_in)
+        skips = jnp.where(first, skip[lo], skip[hi])
+        gated = (scanned + skips * xf) * (gate / (1.0 + jnp.exp(-gate)))
+        sq = gated * gated
+        sq_hi = sq.astype(BF16)
+        sq_lo = (sq - sq_hi.astype(F32)).astype(BF16)
+        meansq = dot_nn(sq_hi, same) + dot_nn(sq_lo, same)
+        normed = (gated * lax.rsqrt(meansq + 1e-05) * gain[:, cols]).astype(BF16)
+        upper, under = normed[:128], normed[128:]
+        nbuf[z, k, :, half] = jnp.where(c == 0, upper, under)
+        ns[k] = jnp.where(c == 0, under, upper)
+        dst = nbuf.at[z, k, :, half]
+        nc[k, "pd"] = send(ns.at[k], dst, dev(y, m4(z + 1), x, 1 - c))
+        nc[k, "md"] = send(ns.at[k], dst, dev(y, m4(z + 3), x, 1 - c))
+        nc[k, "pc"] = send(dst, dst, zp)
+        nc[k, "mc"] = send(dst, dst, zm)
+        nc[k, "s"] = send(ns.at[k], dst, sib)
+
+    def final():
+        ecum = fa["ecum"]
+        rows_first = lax.broadcasted_iota(jnp.int32, (128, 256), 0) < 64
+        for k in range(4):
+            cols = slice(128 * k, 128 * k + 128)
+            lo, hi = 2 * k, 2 * k + 1
             last = jnp.where(rows_first, ecum[255:256, lo : lo + 1], ecum[255:256, hi : hi + 1])
-            fin_out[128 * k : 128 * k + 128, :] = last * s_in.astype(F32) + dot_tn(weighted, bmat)
-
-    def nf():
+            fin_out[cols, :] = last * start[cols, :].astype(F32) + dot_tn(wt[:, cols], bc[0])
+
+    def nf(j):
+        for k in (2 * j, 2 * j + 1):
+            nc[k, "pc"].wait_recv()
+            nc[k, "pd"].wait_recv()
+        fw = nbuf.at[m4(z + 3), pl.ds(2 * j, 2), pl.ds(0, 64)]
+        nc[j, "fp"] = send(fw, fw, zp)
+        for k in (2 * j, 2 * j + 1):
+            nc[k, "mc"].wait_recv()
+            nc[k, "md"].wait_recv()
+        fw = nbuf.at[m4(z + 1), pl.ds(2 * j, 2), pl.ds(64, 64)]
+        nc[j, "fm"] = send(fw, fw, zm)
+
+    def ng():
+        for j in range(2):
+            nc[j, "fp"].wait_recv()
+            nc[j, "fm"].wait_recv()
+
+    def nw():
         for k in range(4):
-            nc[k, "p"].wait_recv()
-            fw = nb.at[m4(z + 3), pl.ds(0, 128), pl.ds(128 * k, 128)]
-            nc[k, "fp"] = send(fw, fw, zp)
-            nc[k, "m"].wait_recv()
-            fw = nb.at[m4(z + 1), pl.ds(128, 128), pl.ds(128 * k, 128)]
-            nc[k, "fm"] = send(fw, fw, zm)
-
-    def ng():
-        for k in range(4):
-            nc[k, "fp"].wait_recv()
-            nc[k, "fm"].wait_recv()
+            nc[k, "s"].wait_recv()
 
     xc = {}
     fr_sem = take(4)
     fin_copies = []
 
     def oa(rr):
-        n = nb[m4(z + rr)]
-        for ii in (2, 1, 3, 0):
-            o = dot_nt(wo[m4(x + ii)], n)
-            left, right = o[:, :128], o[:, 128:]
-            keep[rr, ii] = jnp.where(c == 0, left, right)
-            cs[rr, ii] = jnp.where(c == 0, right, left).astype(BF16)
-        xc[rr, "c"] = send(cs.at[rr], cr.at[rr], sib)
-
-    def ob(rr):
-        xc[rr, "c"].wait_recv()
-        o2[rr] = (keep[rr, 2] + cr[rr, 2].astype(F32)).astype(BF16)
+        zr = m4(z + rr)
+
+        def prod(ii):
+            i = m4(x + ii)
+            o = dot_nt(wo[i, 0], nbuf[zr, 0])
+            for k in range(1, 4):
+                o = o + dot_nt(wo[i, k], nbuf[zr, k])
+            return o
+
+        o2[rr] = prod(2).astype(BF16)
         xc[rr, "2a"] = send(o2.at[rr, pl.ds(0, 160)], e2a.at[rr], xp)
         xc[rr, "2b"] = send(o2.at[rr, pl.ds(160, 160)], e2b.at[rr], xm)
-        o1[rr, 160:] = (keep[rr, 1, 160:] + cr[rr, 1, 160:].astype(F32)).astype(BF16)
+        o = prod(1)
+        k1[rr] = o[:160]
+        o1[rr, 160:] = o[160:].astype(BF16)
         xc[rr, "1ah"] = send(o1.at[rr, pl.ds(160, 160)], e1a.at[rr, pl.ds(160, 160)], xp)
-        o3[rr, :160] = (keep[rr, 3, :160] + cr[rr, 3, :160].astype(F32)).astype(BF16)
+        o = prod(3)
+        k3[rr] = o[160:]
+        o3[rr, :160] = o[:160].astype(BF16)
         xc[rr, "1bl"] = send(o3.at[rr, pl.ds(0, 160)], e1b.at[rr, pl.ds(0, 160)], xm)
+        k0[rr] = prod(0)
 
     def od(rr):
         xc[rr, "2a"].wait_recv()
-        o1[rr, :160] = (keep[rr, 1, :160] + cr[rr, 1, :160].astype(F32) + e2a[rr].astype(F32)).astype(BF16)
+        o1[rr, :160] = (k1[rr] + e2a[rr].astype(F32)).astype(BF16)
         xc[rr, "1al"] = send(o1.at[rr, pl.ds(0, 160)], e1a.at[rr, pl.ds(0, 160)], xp)
         xc[rr, "2b"].wait_recv()
-        o3[rr, 160:] = (keep[rr, 3, 160:] + cr[rr, 3, 160:].astype(F32) + e2b[rr].astype(F32)).astype(BF16)
+        o3[rr, 160:] = (k3[rr] + e2b[rr].astype(F32)).astype(BF16)
         xc[rr, "1bh"] = send(o3.at[rr, pl.ds(160, 160)], e1b.at[rr, pl.ds(160, 160)], xm)
 
     def oe(rr):
         for k in ("1ah", "1bl", "1al", "1bh"):
             xc[rr, k].wait_recv()
-        total = keep[rr, 0] + cr[rr, 0].astype(F32) + e1a[rr].astype(F32) + e1b[rr].astype(F32)
+        total = k0[rr] + e1a[rr].astype(F32) + e1b[rr].astype(F32)
         fs[rr] = total.astype(BF16)
         dst = mt.at[pl.ds(mo(sz * 320, 64), 320), pl.ds(mo(c * 128, 128), 128)]
         cp = copy_of(fs.at[rr], dst, dev(y, m4(z + rr), x, zc), take(), fr_sem + 2 * sz + c)
@@ -497,79 +664,49 @@
 
         mix_out[...] = mt[...]
 
-    h0()
-    w0(0)
-    s0(1)
-    w_init()
-    hs(2)
-    hs(1)
-    hs(3)
-    hs(0)
-    hf(2)
-    hf(1)
-    wf(0)
-    w0(1)
-    hf(3)
-    hg(2)
-    hf(0)
-    hg(1)
-    hg(3)
-    hg(0)
-    wg(0)
-    hw(2)
-    pa(0)
-    hw(1)
-    hw(3)
-    s1(1)
-    pb(0)
-    wf(1)
-    w0(2)
-    hw(0)
-    wg(1)
-    pa(1)
-    pd(0)
-    m0()
-    wf(2)
-    s0(0)
-    pb(1)
-    wg(2)
-    pa(2)
-    s2(1)
-    pd(1)
-    pb(2)
-    s3(1)
-    s1(0)
-    pd(2)
-    s4(1)
-    wo0()
-    s2(0)
-    s3(0)
-    wof()
-    s4(0)
-    mw()
-    scan()
-    wog()
-    oa(0)
-    nf()
-    ob(0)
-    oa(1)
-    od(0)
-    ob(1)
-    oa(3)
-    od(1)
-    ob(3)
-    oe(0)
-    ng()
-    oa(2)
-    od(3)
-    ob(2)
-    oe(1)
-    oe(3)
-    od(2)
-    oe(2)
-    of()
+    steps = dict(
+        h0=h0,
+        hf=hf,
+        hg=hg,
+        hs=hs,
+        hw=hw,
+        m0=m0,
+        mw=mw,
+        nf=nf,
+        ng=ng,
+        nw=nw,
+        oa=oa,
+        od=od,
+        oe=oe,
+        of=of,
+        pa=pa,
+        pb=pb,
+        pd=pd,
+        s0=s0,
+        s1=s1,
+        s2=s2,
+        s3=s3,
+        s4=s4,
+        scan_a=scan_a,
+        scan_b=scan_b,
+        final=final,
+        w0=w0,
+        w_cat=w_cat,
+        w_init=w_init,
+        wf=wf,
+        wg=wg,
+        wo0=wo0,
+        wof=wof,
+        wog=wog,
+        wow=wow,
+    )
+    for step in ORDER:
+        name, *args = step.split()
+        steps[name](*map(int, args))
 
     for cp in sent:
+        cp.finish()
+    for cp in map_copies:
         cp.wait_send()
     for local, cp in h0_local:
 
@@ -587,24 +724,16 @@
             cp.wait_send()
 
 
+def finish_body(mixed_t, final, mixed_out, final_out):
+    mixed_out[...] = mixed_t[...].T
+    final_out[...] = final[...]
+
+
 def shards(hidden, snap_map, pool_states, w_zx, w_bc, w_dt, dt_bias, decay_rate, skip, norm_gain, w_out):
-    h = lax.axis_index("head")
-    c = lax.rem(h, 2)
-    w_b = lax.dynamic_slice_in_dim(w_bc, h * 64, 64, axis=1)
-    w_d = jnp.pad(w_dt, ((0, 0), (0, 56)))
-    tile = jnp.where(c == 0, jnp.concatenate([w_b, w_d], 1), jnp.concatenate([w_d, w_b], 1))
-    wcat = jnp.concatenate([tile, w_zx.reshape(320, 1024)], axis=1)
-    small = jnp.stack(
-        [
-            jnp.pad(dt_bias, (0, 504)),
-            jnp.pad(decay_rate, (0, 504)),
-            jnp.repeat(skip, 64),
-            norm_gain,
-        ]
-        + [jnp.zeros((512,), F32)] * 4
-    )
     vm = pl.BlockSpec(memory_space=VMEM)
+    sm = pl.BlockSpec(memory_space=pltpu.SMEM)
     scratch = [
+        VMEM((320, 3 * CH), BF16),
         VMEM((1024, 1536), BF16),
         VMEM((1536, 3 * CH), BF16),
         *[VMEM((3, 256, CH), BF16)] * 3,
@@ -618,10 +747,14 @@
         *[VMEM((2, 128, 256), BF16)] * 4,
         *[VMEM((2, 256, 256), BF16)] * 2,
         VMEM((512, 256), BF16),
-        VMEM((4, 256, 512), BF16),
-        VMEM((4, 320, 512), BF16),
-        VMEM((4, 4, 320, 128), F32),
-        *[VMEM((4, 4, 320, 128), BF16)] * 2,
+        VMEM((256, 512), F32),
+        VMEM((256, 512), BF16),
+        VMEM((2, 256, 256), BF16),
+        VMEM((4, 128, 128), BF16),
+        VMEM((4, 4, 128, 256), BF16),
+        VMEM((4, 4, 320, 256), BF16),
+        VMEM((4, 320, 128), F32),
+        *[VMEM((4, 160, 128), F32)] * 2,
         *[VMEM((4, 320, 128), BF16)] * 3,
         *[VMEM((4, 160, 128), BF16)] * 2,
         *[VMEM((4, 320, 128), BF16)] * 3,
@@ -632,14 +765,32 @@
     mixed_t, final = pl.pallas_call(
         body,
         out_shape=(jax.ShapeDtypeStruct((640, 256), BF16), jax.ShapeDtypeStruct((512, 256), F32)),
-        in_specs=[pl.BlockSpec(memory_space=pltpu.SMEM)] + [vm] * 5,
+        in_specs=[sm] * 4 + [vm] * 7,
         out_specs=(vm, vm),
         scratch_shapes=scratch,
         compiler_params=pltpu.CompilerParams(
             collective_id=0, has_side_effects=True, vmem_limit_bytes=56 * 1024 * 1024
         ),
-    )(snap_map, hidden.reshape(256, 640), wcat, w_out.T, pool_states.reshape(8, 512, 256), small)
-    return mixed_t.T.reshape(1, 256, 640), final.reshape(1, 8, 64, 256)
+    )(
+        snap_map,
+        dt_bias,
+        decay_rate,
+        skip,
+        norm_gain.reshape(1, 512),
+        hidden.reshape(256, 640),
+        w_zx,
+        w_bc,
+        w_dt.T,
+        w_out.T,
+        pool_states.reshape(8, 512, 256),
+    )
+    mixed, final = pl.pallas_call(
+        finish_body,
+        out_shape=(jax.ShapeDtypeStruct((256, 640), BF16), jax.ShapeDtypeStruct((512, 256), F32)),
+        in_specs=[vm, vm],
+        out_specs=(vm, vm),
+    )(mixed_t, final)
+    return mixed.reshape(1, 256, 640), final.reshape(1, 8, 64, 256)
 
 
 def solution(mesh):

time: 129 us -> 108 us (0.84)
  local copies, waits for them, and re-layouts: 9.34 us -> 0 us
  Pallas kernels: 117 us -> 108 us
    pallas_call x1, Pallas kernels: 117 us -> 105 us  [shards(): pl.pallas_call(body, out_shape=(jax.ShapeDtypeStruct((640, 256), BF16), j...]
    unnamed x6 -> x0, local copies, waits for them, and re-layouts: 5.75 us -> none
    pallas_call x0 -> x1, Pallas kernels: none -> 2.14 us  [shards(): pl.pallas_call(finish_body, out_shape=(jax.ShapeDtypeStruct((256, 640), B...]
    another operation x3 -> x0, local copies, waits for them, and re-layouts: 1.39 us -> none  [shards(): jnp.stack([jnp.pad(dt_bias, (0, 504)), jnp.pad(decay_rate, (0, 504)), jnp...]
    pad x3 -> x0, local copies, waits for them, and re-layouts: 1.39 us -> none  [the longest x1 0.7 us: shards(): jnp.pad(dt_bias, (0, 504))]
where the time goes in v2:
time: 108 us
  Pallas kernels  108 us (100%)
    pallas_call x1, Pallas kernels, shards(): pl.pallas_call(body, out_shape=(jax.ShapeDtypeStruct((640, 256), BF16), j...  105 us

profile of v2, /device:TPU:1, one launch (start us, length us, event | category | flops | bytes accessed | tf_op | source)
XLA Modules:
  0.0 108.3 jit_solution(12672318565751538357)
XLA Ops:
  0.6 105.5 %shard_map.122 = (bf16[640,256]{1,0:T(8,128)(2,1)}, f32[512,256]{1,0:T(8,128)}) custom-call(s32[16]{0:T(128)} %snap.1, f32[8]{0:T(128)} %bias.1, f32[8]{0:T(128)} %rate.1, f32[8]{0:T(128)} %skip.1, f32[1,512]{1,0:T(1,128)} %bitcast.11, bf16[256,640]{1,0:T(8,128)(2,1)} %bitcast.8, bf16[320,2,512]{2,1,0:T(2,128)(2,1)} %wzx.1, bf16[320,512]{1,0:T(8,128)(2,1)} %wbc.1, ...), custom_call_target="tpu_custom_call" | custom-call | tf_op jit(solution)/shard_map/pallas_call | solution.py:765
  106.1 2.1 %shard_map.123 = (bf16[256,640]{1,0:T(8,128)(2,1)}, f32[512,256]{1,0:T(8,128)}) custom-call(bf16[640,256]{1,0:T(8,128)(2,1)} %get-tuple-element.6.mixed_t, f32[512,256]{1,0:T(8,128)} %get-tuple-element.7.final), custom_call_target="tpu_custom_call" | custom-call | tf_op jit(solution)/shard_map/pallas_call | solution.py:787

commit v3 on v2

--- a/solution.py
+++ b/solution.py
@@ -11,85 +11,88 @@
 VMEM = pltpu.VMEM
 
 N_SEM = 176
+ROWS = (192, 320)
+FIRST_ROW = (0, 192)
 CH = 384
 
 
 ORDER = (
     "h0",
     "w_cat",
-    "w0 0",
-    "s0 1",
     "w0 1",
     "w0 2",
+    "s0 1",
+    "hs 3",
+    "hs 1",
+    "wf 1",
+    "w0 0",
+    "hs 2",
+    "hs 0",
+    "wf 2",
+    "s1 1",
+    "hf 3",
+    "hf 2",
+    "hf 0",
+    "hf 1",
+    "hg 2",
+    "wg 1",
+    "wf 0",
+    "hw 2",
+    "s0 0",
+    "hg 3",
     "w_init",
-    "s0 0",
-    "hs 2",
-    "hs 1",
-    "hs 3",
-    "hs 0",
-    "hf 2",
-    "hf 1",
-    "wf 0",
-    "hf 3",
-    "hg 2",
-    "hf 0",
+    "pa 1",
     "hg 1",
-    "hg 3",
+    "hw 3",
+    "wg 2",
+    "hw 1",
+    "wg 0",
     "hg 0",
-    "s1 1",
-    "wf 1",
-    "wg 0",
-    "hw 2",
     "pa 0",
-    "hw 1",
-    "hw 3",
-    "pb 0",
-    "wf 2",
+    "pb1 0",
+    "pa 2",
+    "s1 0",
+    "s2 1",
+    "pb2 0",
+    "pb1 1",
+    "pb1 2",
+    "pb2 1",
     "hw 0",
-    "wg 1",
-    "pa 1",
+    "wo0",
     "pd 0",
     "m0",
-    "s1 0",
-    "pb 1",
-    "wg 2",
-    "pa 2",
-    "s2 1",
+    "s2 0",
+    "pb2 2",
+    "s3 1",
     "pd 1",
-    "pb 2",
-    "s3 1",
-    "s2 0",
+    "mw",
+    "scan_a",
+    "wof",
     "pd 2",
-    "mw",
-    "wo0",
-    "scan_a",
+    "s4 0",
     "s4 1",
-    "s3 0",
-    "wof",
-    "s4 0",
     "scan_b 0",
     "scan_b 1",
     "scan_b 2",
     "scan_b 3",
     "wog",
+    "nf 0",
     "nw",
     "wow",
     "oa 0",
-    "nf 0",
     "nf 1",
-    "od 0",
     "oa 1",
     "oa 3",
+    "od 1",
+    "final",
     "ng",
-    "oe 0",
-    "oa 2",
-    "od 1",
+    "o_far",
     "od 3",
-    "od 2",
+    "od 0",
     "oe 1",
     "oe 3",
-    "oe 2",
-    "final",
+    "far_in",
+    "oe 0",
     "of",
 )
 
@@ -147,6 +150,8 @@
     r2b,
     r1a,
     r1b,
+    ka,
+    kb,
     pz,
     maps,
     f2,
@@ -157,12 +162,11 @@
     q2b,
     q1a,
     q1b,
+    v2,
+    v1a,
+    v1b,
     g1,
     g3,
-    v2a,
-    v2b,
-    v1a,
-    v1b,
     start,
     wi,
     wt,
@@ -170,6 +174,8 @@
     ns,
     nbuf,
     wo,
+    d2,
+    h2,
     k0,
     k1,
     k3,
@@ -232,6 +238,7 @@
     peers = [(p, lax.rem(h + i, 8)) for i in range(1, 8)]
     peers += [dev(y, m4(z + i), x, cc) for i in range(1, 4) for cc in range(2)]
     peers += [yp, ym]
+    peers += [dev(y, m4(z + 2), m4(x + i), cc) for i in range(1, 4) for cc in range(2)]
     for peer in peers:
         pl.semaphore_signal(barrier, inc=1, device_id=peer, device_id_type=MESH)
     pl.semaphore_wait(barrier, len(peers))
@@ -316,8 +323,8 @@
         steps_w = dot_tn(wdt[...], place).astype(BF16)
         maps_w = wbc[:, pl.ds(mo(x * 128, 128), 128)]
         wcat[:, :128] = jnp.where(lane // 64 == c, maps_w, steps_w)
-        wcat[:, 128:640] = wzx[:, 0, :]
-        wcat[:, 640:] = wzx[:, 1, :]
+        wcat[:, 128:640] = wzx[:, 1, :]
+        wcat[:, 640:] = wzx[:, 0, :]
 
     def w_init():
         for i in range(4):
@@ -353,18 +360,22 @@
         pc[n, "2a"] = send(p2.at[n, pl.ds(0, 128)], r2a.at[n], zp)
         pc[n, "2b"] = send(p2.at[n, pl.ds(128, 128)], r2b.at[n], zm)
 
-    def pb(n):
+    def pb1(n):
         a = part(n, 1)
         p1[n, 128:] = a[128:].astype(BF16)
         pc[n, "1ah"] = send(p1.at[n, pl.ds(128, 128)], r1a.at[n, pl.ds(128, 128)], zp)
+        ka[n] = a[:128]
         b = part(n, 3)
         p3[n, :128] = b[:128].astype(BF16)
         pc[n, "1bl"] = send(p3.at[n, pl.ds(0, 128)], r1b.at[n, pl.ds(0, 128)], zm)
+        kb[n] = b[128:]
+
+    def pb2(n):
         pc[n, "2a"].wait_recv()
-        p1[n, :128] = (a[:128] + r2a[n].astype(F32)).astype(BF16)
+        p1[n, :128] = (ka[n] + r2a[n].astype(F32)).astype(BF16)
         pc[n, "1al"] = send(p1.at[n, pl.ds(0, 128)], r1a.at[n, pl.ds(0, 128)], zp)
         pc[n, "2b"].wait_recv()
-        p3[n, 128:] = (b[128:] + r2b[n].astype(F32)).astype(BF16)
+        p3[n, 128:] = (kb[n] + r2b[n].astype(F32)).astype(BF16)
         pc[n, "1bh"] = send(p3.at[n, pl.ds(128, 128)], r1b.at[n, pl.ds(128, 128)], zm)
 
     def pd(n):
@@ -391,37 +402,38 @@
 
     sc = {}
     axes = (((y, yp, ym), (z, zp, zm)), ((z, zp, zm), (y, yp, ym)))
-
-    def pick(half, a, b):
-        r = a * 4 + b if half == 0 else b * 4 + a
+    far2 = (dev(y, m4(z + 2), x, c), None)
+
+    def pick(u, a, b):
+        r = a * 4 + b if u == 0 else b * 4 + a
         idx = snap[r]
-        v = pool[lax.rem(idx, 8), half * 256 : half * 256 + 256, :]
+        v = pool[lax.rem(idx, 8), FIRST_ROW[u] : FIRST_ROW[u] + ROWS[u], :]
         return jnp.where(idx // 8 == p, v, jnp.zeros_like(v))
 
     def s0(u):
         (a, ap, am), _ = axes[u]
         for b in range(4):
-            f2[u, b] = pick(u, m4(a + 2), b)
+            f2[u][b] = pick(u, m4(a + 2), b)
             if b == 1:
-                sc[u, "2a"] = send(f2.at[u, pl.ds(0, 2)], q2a.at[u], ap)
-        sc[u, "2b"] = send(f2.at[u, pl.ds(2, 2)], q2b.at[u], am)
+                sc[u, "2a"] = send(f2[u].at[pl.ds(0, 2)], q2a[u], ap)
+        sc[u, "2b"] = send(f2[u].at[pl.ds(2, 2)], q2b[u], am)
         for b in (2, 3):
-            f1[u, b] = pick(u, m4(a + 1), b)
-        sc[u, "1ah"] = send(f1.at[u, pl.ds(2, 2)], q1a.at[u, pl.ds(2, 2)], ap)
+            f1[u][b] = pick(u, m4(a + 1), b)
+        sc[u, "1ah"] = send(f1[u].at[pl.ds(2, 2)], q1a[u].at[pl.ds(2, 2)], ap)
         for b in (0, 1):
-            f3[u, b] = pick(u, m4(a + 3), b)
-        sc[u, "1bl"] = send(f3.at[u, pl.ds(0, 2)], q1b.at[u, pl.ds(0, 2)], am)
+            f3[u][b] = pick(u, m4(a + 3), b)
+        sc[u, "1bl"] = send(f3[u].at[pl.ds(0, 2)], q1b[u].at[pl.ds(0, 2)], am)
 
     def s1(u):
         (a, ap, am), _ = axes[u]
         sc[u, "2a"].wait_recv()
         for b in (0, 1):
-            f1[u, b] = pick(u, m4(a + 1), b) + q2a[u, b]
-        sc[u, "1al"] = send(f1.at[u, pl.ds(0, 2)], q1a.at[u, pl.ds(0, 2)], ap)
+            f1[u][b] = pick(u, m4(a + 1), b) + q2a[u][b]
+        sc[u, "1al"] = send(f1[u].at[pl.ds(0, 2)], q1a[u].at[pl.ds(0, 2)], ap)
         sc[u, "2b"].wait_recv()
         for b in (2, 3):
-            f3[u, b] = pick(u, m4(a + 3), b) + q2b[u, b - 2]
-        sc[u, "1bh"] = send(f3.at[u, pl.ds(2, 2)], q1b.at[u, pl.ds(2, 2)], am)
+            f3[u][b] = pick(u, m4(a + 3), b) + q2b[u][b - 2]
+        sc[u, "1bh"] = send(f3[u].at[pl.ds(2, 2)], q1b[u].at[pl.ds(2, 2)], am)
 
     def s2(u):
         (a, _, _), (b0, bp, bm) = axes[u]
@@ -430,28 +442,41 @@
         sc[u, "1al"].wait_recv()
         sc[u, "1bh"].wait_recv()
         for b in range(4):
-            tt[u, b] = pick(u, a, b) + q1a[u, b] + q1b[u, b]
+            tt[u][b] = pick(u, a, b) + q1a[u][b] + q1b[u][b]
         far, nxt, prv = m4(b0 + 2), m4(b0 + 1), m4(b0 + 3)
-        sc[u, "v2a"] = send(tt.at[u, far, pl.ds(0, 128)], v2a.at[u], bp)
-        sc[u, "v2b"] = send(tt.at[u, far, pl.ds(128, 128)], v2b.at[u], bm)
-        sc[u, "v1ah"] = send(tt.at[u, nxt, pl.ds(128, 128)], v1a.at[u, pl.ds(128, 128)], bp)
-        sc[u, "v1bl"] = send(tt.at[u, prv, pl.ds(0, 128)], v1b.at[u, pl.ds(0, 128)], bm)
+        if far2[u] is not None:
+            sc[u, "v2"] = send(tt[u].at[far], v2[u], far2[u])
+            sc[u, "v1a"] = send(tt[u].at[nxt], v1a[u], bp)
+            sc[u, "v1b"] = send(tt[u].at[prv], v1b[u], bm)
+            return
+        n = ROWS[u] // 2
+        sc[u, "v2a"] = send(tt[u].at[far, pl.ds(0, n)], v2[u].at[pl.ds(0, n)], bp)
+        sc[u, "v2b"] = send(tt[u].at[far, pl.ds(n, n)], v2[u].at[pl.ds(n, n)], bm)
+        sc[u, "v1ah"] = send(tt[u].at[nxt, pl.ds(n, n)], v1a[u].at[pl.ds(n, n)], bp)
+        sc[u, "v1bl"] = send(tt[u].at[prv, pl.ds(0, n)], v1b[u].at[pl.ds(0, n)], bm)
 
     def s3(u):
         _, (b0, bp, bm) = axes[u]
         nxt, prv = m4(b0 + 1), m4(b0 + 3)
+        n = ROWS[u] // 2
         sc[u, "v2a"].wait_recv()
-        g1[u] = tt[u, nxt, :128, :] + v2a[u]
-        sc[u, "v1al"] = send(g1.at[u], v1a.at[u, pl.ds(0, 128)], bp)
+        g1[...] = tt[u][nxt, :n, :] + v2[u][:n]
+        sc[u, "v1al"] = send(g1, v1a[u].at[pl.ds(0, n)], bp)
         sc[u, "v2b"].wait_recv()
-        g3[u] = tt[u, prv, 128:, :] + v2b[u]
-        sc[u, "v1bh"] = send(g3.at[u], v1b.at[u, pl.ds(128, 128)], bm)
+        g3[...] = tt[u][prv, n:, :] + v2[u][n:]
+        sc[u, "v1bh"] = send(g3, v1b[u].at[pl.ds(n, n)], bm)
 
     def s4(u):
         _, (b0, _, _) = axes[u]
+        rows = slice(FIRST_ROW[u], FIRST_ROW[u] + ROWS[u])
+        if far2[u] is not None:
+            for k in ("v2", "v1a", "v1b"):
+                sc[u, k].wait_recv()
+            start[rows] = tt[u][b0] + v1a[u][...] + v1b[u][...] + v2[u][...]
+            return
         for k in ("v1ah", "v1bl", "v1al", "v1bh"):
             sc[u, k].wait_recv()
-        start[u * 256 : u * 256 + 256] = tt[u, b0] + v1a[u] + v1b[u]
+        start[rows] = tt[u][b0] + v1a[u][...] + v1b[u][...]
 
     oc = {}
     half = pl.ds(mo(c * 128, 128), 128)
@@ -523,7 +548,7 @@
             bc[1, :, 128 * i : 128 * i + 128] = jnp.where(first, maps[4 + 2 * i], maps[5 + 2 * i])
         scores = dot_nt(bc[1], bc[0])
         for k in range(4):
-            xv = pz[:, 640 + 128 * k : 768 + 128 * k]
+            xv = pz[:, 128 + 128 * k : 256 + 128 * k]
 
             def within(q):
                 spread = jnp.where(lower, cum[:, q : q + 1] - cum_t[q : q + 1, :], -1e30)
@@ -544,8 +569,8 @@
         r128 = lax.broadcasted_iota(jnp.int32, (128, 128), 0) // 64
         c128 = lax.broadcasted_iota(jnp.int32, (128, 128), 1) // 64
         same = jnp.where(r128 == c128, 1.0 / 64.0, 0.0).astype(BF16)
-        xf = pz[:, 640 + 128 * k : 768 + 128 * k].astype(F32)
-        gate = pz[:, 128 + 128 * k : 256 + 128 * k].astype(F32)
+        xf = pz[:, 128 + 128 * k : 256 + 128 * k].astype(F32)
+        gate = pz[:, 640 + 128 * k : 768 + 128 * k].astype(F32)
         s_in = start[cols, :]
         decay = jnp.where(first, ecum[:, lo : lo + 1], ecum[:, hi : hi + 1])
         scanned = wi[:, cols] + decay * dot_nt(bc[1], s_in)
@@ -600,15 +625,39 @@
     fr_sem = take(4)
     fin_copies = []
 
+    def out_prod(zr, i):
+        o = dot_nt(wo[i, 0], nbuf[zr, 0])
+        for k in range(1, 4):
+            o = o + dot_nt(wo[i, k], nbuf[zr, k])
+        return o
+
+    d_sem = take(8)
+    direct = []
+
+    def o_far():
+        for ii in (2, 1, 3, 0):
+            i = m4(x + ii)
+            d2[ii] = out_prod(m4(z + 2), i).astype(BF16)
+            cp = copy_of(d2.at[ii], h2.at[2 * ii + c], dev(y, m4(z + 2), i, zc), take(), d_sem + 2 * ii + c)
+            cp.start()
+            direct.append(cp)
+
+    def far_in():
+        @pl.when(c == m4(z + 2) // 2)
+        def _():
+            for cc in range(2):
+                total = jnp.zeros((320, 128), F32)
+                for ii in (0, 1, 3, 2):
+                    q = 2 * ii + cc
+                    copy_of(h2.at[q], h2.at[q], sib, hs_sem, d_sem + q).wait_recv()
+                    total = total + h2[q].astype(F32)
+                mt[pl.ds(mo(sz * 320, 64), 320), 128 * cc : 128 * cc + 128] = total.astype(BF16)
+
     def oa(rr):
         zr = m4(z + rr)
 
         def prod(ii):
-            i = m4(x + ii)
-            o = dot_nt(wo[i, 0], nbuf[zr, 0])
-            for k in range(1, 4):
-                o = o + dot_nt(wo[i, k], nbuf[zr, k])
-            return o
+            return out_prod(zr, m4(x + ii))
 
         o2[rr] = prod(2).astype(BF16)
         xc[rr, "2a"] = send(o2.at[rr, pl.ds(0, 160)], e2a.at[rr], xp)
@@ -656,7 +705,7 @@
             for cc in range(2):
                 dst = mt.at[pl.ds(s * 320, 320), pl.ds(cc * 128, 128)]
                 got = copy_of(dst, dst, sib, hs_sem, fr_sem + 2 * s + cc)
-                local = (z == 2 * c + s) & (c == cc)
+                local = ((z == 2 * c + s) & (c == cc)) | (m4(z + 2) == 2 * c + s)
 
                 @pl.when(jnp.logical_not(local))
                 def _(got=got):
@@ -679,8 +728,11 @@
         od=od,
         oe=oe,
         of=of,
+        o_far=o_far,
+        far_in=far_in,
         pa=pa,
-        pb=pb,
+        pb1=pb1,
+        pb2=pb2,
         pd=pd,
         s0=s0,
         s1=s1,
@@ -706,7 +758,7 @@
 
     for cp in sent:
         cp.finish()
-    for cp in map_copies:
+    for cp in map_copies + direct:
         cp.wait_send()
     for local, cp in h0_local:
 
@@ -739,13 +791,14 @@
         *[VMEM((3, 256, CH), BF16)] * 3,
         *[VMEM((3, 128, CH), BF16)] * 2,
         *[VMEM((3, 256, CH), BF16)] * 2,
+        *[VMEM((3, 128, CH), F32)] * 2,
         VMEM((256, 3 * CH), BF16),
         VMEM((8, 256, 128), BF16),
-        *[VMEM((2, 4, 256, 256), BF16)] * 4,
-        *[VMEM((2, 2, 256, 256), BF16)] * 2,
-        *[VMEM((2, 4, 256, 256), BF16)] * 2,
-        *[VMEM((2, 128, 256), BF16)] * 4,
-        *[VMEM((2, 256, 256), BF16)] * 2,
+        *[tuple(VMEM((4, n, 256), BF16) for n in ROWS)] * 4,
+        *[tuple(VMEM((2, n, 256), BF16) for n in ROWS)] * 2,
+        *[tuple(VMEM((4, n, 256), BF16) for n in ROWS)] * 2,
+        *[tuple(VMEM((n, 256), BF16) for n in ROWS)] * 3,
+        *[VMEM((ROWS[1] // 2, 256), BF16)] * 2,
         VMEM((512, 256), BF16),
         VMEM((256, 512), F32),
         VMEM((256, 512), BF16),
@@ -753,6 +806,8 @@
         VMEM((4, 128, 128), BF16),
         VMEM((4, 4, 128, 256), BF16),
         VMEM((4, 4, 320, 256), BF16),
+        VMEM((4, 320, 128), BF16),
+        VMEM((8, 320, 128), BF16),
         VMEM((4, 320, 128), F32),
         *[VMEM((4, 160, 128), F32)] * 2,
         *[VMEM((4, 320, 128), BF16)] * 3,

time: 108 us -> 96 us (0.89)
  Pallas kernels: 108 us -> 95.2 us
    pallas_call x1, Pallas kernels: 105 us -> 93.1 us  [shards(): pl.pallas_call(body, out_shape=(jax.ShapeDtypeStruct((640, 256), BF16), j...]
where the time goes in v3:
time: 96 us; the launch traced here: 95.9 us
  Pallas kernels  95.2 us (99%)
    pallas_call x1, Pallas kernels, shards(): pl.pallas_call(body, out_shape=(jax.ShapeDtypeStruct((640, 256), BF16), j...  93.1 us
    pallas_call x1, Pallas kernels, shards(): pl.pallas_call(finish_body, out_shape=(jax.ShapeDtypeStruct((256, 640), B...  2.14 us

profile of v3, /device:TPU:1, one launch (start us, length us, event | category | flops | bytes accessed | tf_op | source)
XLA Modules:
  0.0 95.9 jit_solution(8407351806717096780)
XLA Ops:
  0.6 93.1 %shard_map.122 = (bf16[640,256]{1,0:T(8,128)(2,1)}, f32[512,256]{1,0:T(8,128)}) custom-call(s32[16]{0:T(128)} %snap.1, f32[8]{0:T(128)} %bias.1, f32[8]{0:T(128)} %rate.1, f32[8]{0:T(128)} %skip.1, f32[1,512]{1,0:T(1,128)} %bitcast.11, bf16[256,640]{1,0:T(8,128)(2,1)} %bitcast.8, bf16[320,2,512]{2,1,0:T(2,128)(2,1)} %wzx.1, bf16[320,512]{1,0:T(8,128)(2,1)} %wbc.1, ...), custom_call_target="tpu_custom_call" | custom-call | tf_op jit(solution)/shard_map/pallas_call | solution.py:820
  93.7 2.1 %shard_map.123 = (bf16[256,640]{1,0:T(8,128)(2,1)}, f32[512,256]{1,0:T(8,128)}) custom-call(bf16[640,256]{1,0:T(8,128)(2,1)} %get-tuple-element.6.mixed_t, f32[512,256]{1,0:T(8,128)} %get-tuple-element.7.final), custom_call_target="tpu_custom_call" | custom-call | tf_op jit(solution)/shard_map/pallas_call | solution.py:842

commit v4 on v3

--- a/solution.py
+++ b/solution.py
@@ -18,7 +18,6 @@
 
 ORDER = (
     "h0",
-    "w_cat",
     "w0 1",
     "w0 2",
     "s0 1",
@@ -40,7 +39,6 @@
     "hw 2",
     "s0 0",
     "hg 3",
-    "w_init",
     "pa 1",
     "hg 1",
     "hw 3",
@@ -132,14 +130,19 @@
     rate,
     skip,
     gain,
+    wdt,
+    hid_in,
+    wzx_in,
+    wbc_in,
+    wout_in,
+    pool_in,
+    mix_out,
+    fin_out,
     hid,
     wzx,
     wbc,
-    wdt,
     wout_t,
     pool,
-    mix_out,
-    fin_out,
     wcat,
     xs_,
     ws_,
@@ -190,6 +193,7 @@
     mt,
     ss,
     rs,
+    ls,
 ):
     p = lax.axis_index("pool")
     h = lax.axis_index("head")
@@ -238,10 +242,17 @@
     peers = [(p, lax.rem(h + i, 8)) for i in range(1, 8)]
     peers += [dev(y, m4(z + i), x, cc) for i in range(1, 4) for cc in range(2)]
     peers += [yp, ym]
-    peers += [dev(y, m4(z + 2), m4(x + i), cc) for i in range(1, 4) for cc in range(2)]
     for peer in peers:
         pl.semaphore_signal(barrier, inc=1, device_id=peer, device_id_type=MESH)
-    pl.semaphore_wait(barrier, len(peers))
+
+    loads = [
+        pltpu.make_async_copy(src, dst, ls.at[i])
+        for i, (src, dst) in enumerate(
+            ((wzx_in, wzx), (wbc_in, wbc), (pool_in, pool), (hid_in, hid), (wout_in, wout_t))
+        )
+    ]
+    for load in loads:
+        load.start()
 
     hs_sem = take(4)
     hr_sem = take(4)
@@ -410,18 +421,20 @@
         v = pool[lax.rem(idx, 8), FIRST_ROW[u] : FIRST_ROW[u] + ROWS[u], :]
         return jnp.where(idx // 8 == p, v, jnp.zeros_like(v))
 
+    def s_pick(u):
+        a = axes[u][0][0]
+        for b in range(4):
+            f2[u][b] = pick(u, m4(a + 2), b)
+        for b in (2, 3):
+            f1[u][b] = pick(u, m4(a + 1), b)
+        for b in (0, 1):
+            f3[u][b] = pick(u, m4(a + 3), b)
+
     def s0(u):
         (a, ap, am), _ = axes[u]
-        for b in range(4):
-            f2[u][b] = pick(u, m4(a + 2), b)
-            if b == 1:
-                sc[u, "2a"] = send(f2[u].at[pl.ds(0, 2)], q2a[u], ap)
+        sc[u, "2a"] = send(f2[u].at[pl.ds(0, 2)], q2a[u], ap)
         sc[u, "2b"] = send(f2[u].at[pl.ds(2, 2)], q2b[u], am)
-        for b in (2, 3):
-            f1[u][b] = pick(u, m4(a + 1), b)
         sc[u, "1ah"] = send(f1[u].at[pl.ds(2, 2)], q1a[u].at[pl.ds(2, 2)], ap)
-        for b in (0, 1):
-            f3[u][b] = pick(u, m4(a + 3), b)
         sc[u, "1bl"] = send(f3[u].at[pl.ds(0, 2)], q1b[u].at[pl.ds(0, 2)], am)
 
     def s1(u):
@@ -743,8 +756,6 @@
         scan_b=scan_b,
         final=final,
         w0=w0,
-        w_cat=w_cat,
-        w_init=w_init,
         wf=wf,
         wg=wg,
         wo0=wo0,
@@ -752,6 +763,17 @@
         wog=wog,
         wow=wow,
     )
+    loads[0].wait()
+    loads[1].wait()
+    w_cat()
+    w_init()
+    loads[2].wait()
+    s_pick(1)
+    s_pick(0)
+    loads[3].wait()
+    loads[4].wait()
+    pl.semaphore_wait(barrier, len(peers))
+
     for step in ORDER:
         name, *args = step.split()
         steps[name](*map(int, args))
@@ -785,6 +807,11 @@
     vm = pl.BlockSpec(memory_space=VMEM)
     sm = pl.BlockSpec(memory_space=pltpu.SMEM)
     scratch = [
+        VMEM((256, 640), BF16),
+        VMEM((320, 2, 512), BF16),
+        VMEM((320, 512), BF16),
+        VMEM((320, 512), BF16),
+        VMEM((8, 512, 256), BF16),
         VMEM((320, 3 * CH), BF16),
         VMEM((1024, 1536), BF16),
         VMEM((1536, 3 * CH), BF16),
@@ -816,11 +843,12 @@
         VMEM((640, 256), BF16),
         pltpu.SemaphoreType.DMA((N_SEM,)),
         pltpu.SemaphoreType.DMA((N_SEM,)),
+        pltpu.SemaphoreType.DMA((5,)),
     ]
     mixed_t, final = pl.pallas_call(
         body,
         out_shape=(jax.ShapeDtypeStruct((640, 256), BF16), jax.ShapeDtypeStruct((512, 256), F32)),
-        in_specs=[sm] * 4 + [vm] * 7,
+        in_specs=[sm] * 4 + [vm] * 2 + [pl.BlockSpec(memory_space=pl.ANY)] * 5,
         out_specs=(vm, vm),
         scratch_shapes=scratch,
         compiler_params=pltpu.CompilerParams(
@@ -832,10 +860,10 @@
         decay_rate,
         skip,
         norm_gain.reshape(1, 512),
+        w_dt.T,
         hidden.reshape(256, 640),
         w_zx,
         w_bc,
-        w_dt.T,
         w_out.T,
         pool_states.reshape(8, 512, 256),
     )

time: 96 us -> 93.1 us (0.970)
  Pallas kernels: 95.2 us -> 92.3 us
    pallas_call x1, Pallas kernels: 93.1 us -> 90.2 us  [shards(): pl.pallas_call(body, out_shape=(jax.ShapeDtypeStruct((640, 256), BF16), j...]
where the time goes in v4:
time: 93.1 us; the launch traced here: 92.9 us
  Pallas kernels  92.3 us (99%)
    pallas_call x1, Pallas kernels, shards(): pl.pallas_call(body, out_shape=(jax.ShapeDtypeStruct((640, 256), BF16), j...  90.2 us
    pallas_call x1, Pallas kernels, shards(): pl.pallas_call(finish_body, out_shape=(jax.ShapeDtypeStruct((256, 640), B...  2.14 us

profile of v4, /device:TPU:1, one launch (start us, length us, event | category | flops | bytes accessed | tf_op | source)
XLA Modules:
  0.0 92.9 jit_solution(9912360120451235564)
XLA Ops:
  0.6 90.2 %shard_map.122 = (bf16[640,256]{1,0:T(8,128)(2,1)}, f32[512,256]{1,0:T(8,128)}) custom-call(s32[16]{0:T(128)} %snap.1, f32[8]{0:T(128)} %bias.1, f32[8]{0:T(128)} %rate.1, f32[8]{0:T(128)} %skip.1, f32[1,512]{1,0:T(1,128)} %bitcast.11, bf16[8,320]{1,0:T(8,128)(2,1)} %bitcast.10, bf16[256,640]{1,0:T(8,128)(2,1)} %bitcast.8, bf16[320,2,512]{2,1,0:T(2,128)(2,1)} %wzx_in.1, ...), custom_call_target="tpu_custom_call" | custom-call | tf_op jit(solution)/shard_map/pallas_call | solution.py:848
  90.8 2.1 %shard_map.123 = (bf16[256,640]{1,0:T(8,128)(2,1)}, f32[512,256]{1,0:T(8,128)}) custom-call(bf16[640,256]{1,0:T(8,128)(2,1)} %get-tuple-element.6.mixed_t, f32[512,256]{1,0:T(8,128)} %get-tuple-element.7.final), custom_call_target="tpu_custom_call" | custom-call | tf_op jit(solution)/shard_map/pallas_call | solution.py:870

commit v5 on v4

--- a/solution.py
+++ b/solution.py
@@ -11,83 +11,85 @@
 VMEM = pltpu.VMEM
 
 N_SEM = 176
-ROWS = (192, 320)
-FIRST_ROW = (0, 192)
+ROWS = (160, 352)
+FIRST_ROW = (0, 160)
 CH = 384
 
 
 ORDER = (
+    "s_pick 1",
     "h0",
-    "w0 1",
     "w0 2",
     "s0 1",
+    "w_init",
+    "s_pick 0",
+    "hs 2",
+    "hs 0",
     "hs 3",
+    "w0 1",
+    "hf 2",
+    "wf 0",
+    "hf 3",
+    "hg 2",
     "hs 1",
     "wf 1",
-    "w0 0",
-    "hs 2",
-    "hs 0",
-    "wf 2",
     "s1 1",
-    "hf 3",
-    "hf 2",
-    "hf 0",
-    "hf 1",
-    "hg 2",
-    "wg 1",
-    "wf 0",
     "hw 2",
     "s0 0",
+    "wg 0",
+    "hf 1",
     "hg 3",
+    "hw 3",
+    "pa 0",
+    "wf 2",
+    "wg 1",
     "pa 1",
+    "s1 0",
     "hg 1",
-    "hw 3",
+    "wo0",
+    "hw 1",
+    "hf 0",
+    "pb1 0",
+    "pb1 1",
+    "pb2 0",
+    "pb2 1",
     "wg 2",
-    "hw 1",
-    "wg 0",
+    "s2 1",
+    "pa 2",
     "hg 0",
-    "pa 0",
-    "pb1 0",
-    "pa 2",
-    "s1 0",
-    "s2 1",
-    "pb2 0",
-    "pb1 1",
-    "pb1 2",
-    "pb2 1",
     "hw 0",
-    "wo0",
+    "s2 0",
     "pd 0",
     "m0",
-    "s2 0",
+    "pb1 2",
+    "pd 1",
+    "s3 1",
     "pb2 2",
-    "s3 1",
-    "pd 1",
+    "s4 0",
     "mw",
+    "wof",
     "scan_a",
-    "wof",
+    "s4 1",
     "pd 2",
-    "s4 0",
-    "s4 1",
+    "scan_b 2",
+    "scan_b 1",
     "scan_b 0",
-    "scan_b 1",
-    "scan_b 2",
+    "wog",
     "scan_b 3",
-    "wog",
-    "nf 0",
     "nw",
     "wow",
     "oa 0",
+    "nf 0",
     "nf 1",
     "oa 1",
+    "final",
     "oa 3",
     "od 1",
-    "final",
     "ng",
     "o_far",
     "od 3",
+    "oe 1",
     "od 0",
-    "oe 1",
     "oe 3",
     "far_in",
     "oe 0",
@@ -187,13 +189,16 @@
     o3,
     e2a,
     e2b,
+    e2,
     e1a,
     e1b,
     fs,
     mt,
+    fin,
     ss,
     rs,
     ls,
+    tier,
 ):
     p = lax.axis_index("pool")
     h = lax.axis_index("head")
@@ -239,9 +244,8 @@
         return pl.multiple_of(v, n)
 
     barrier = pltpu.get_barrier_semaphore()
-    peers = [(p, lax.rem(h + i, 8)) for i in range(1, 8)]
-    peers += [dev(y, m4(z + i), x, cc) for i in range(1, 4) for cc in range(2)]
-    peers += [yp, ym]
+    peers = [sib, xp, xm, yp, ym]
+    peers += [dev(y, m4(z + i), x, cc) for i in (1, 3) for cc in range(2)]
     for peer in peers:
         pl.semaphore_signal(barrier, inc=1, device_id=peer, device_id_type=MESH)
 
@@ -261,16 +265,18 @@
     def x_block(req, half_off, rows, xx):
         return xs_.at[pl.ds(mo(req * 256 + half_off, 64), rows), pl.ds(mo(xx * 384, 128), 384)]
 
-    def h0():
+    def h0_near():
         for s in range(2):
             for d in range(2):
-                local = (z == 2 * c + s) & (c == d)
+                zq = 2 * c + s
+                local = (z == zq) & (c == d)
+                far = m4(zq + 4 - z) == 2
                 src = hid.at[pl.ds(d * 128, 128), pl.ds(256 * s, 384)]
                 dst = x_block(z, d * 128, 128, x)
-                cp = copy_of(src, dst, dev(y, 2 * c + s, x, d), hs_sem + 2 * s + d, hr_sem + z)
-                h0_local.append((local, cp))
-
-                @pl.when(jnp.logical_not(local))
+                cp = copy_of(src, dst, dev(y, zq, x, d), hs_sem + 2 * s + d, hr_sem + z)
+                h0_local.append((local, far, cp))
+
+                @pl.when(jnp.logical_not(local | far))
                 def _(cp=cp):
                     cp.start()
 
@@ -279,6 +285,14 @@
                     xs_[pl.ds(mo(z * 256 + d * 128, 64), 128), pl.ds(mo(x * 384, 128), 384)] = hid[
                         d * 128 : d * 128 + 128, 256 * s : 256 * s + 384
                     ]
+
+    def h0():
+        pl.semaphore_wait(tier, 1)
+        for _, far, cp in h0_local:
+
+            @pl.when(far)
+            def _(cp=cp):
+                cp.start()
 
     hc = {}
 
@@ -422,6 +436,8 @@
         return jnp.where(idx // 8 == p, v, jnp.zeros_like(v))
 
     def s_pick(u):
+        if u == 1:
+            loads[2].wait()
         a = axes[u][0][0]
         for b in range(4):
             f2[u][b] = pick(u, m4(a + 2), b)
@@ -495,6 +511,7 @@
     half = pl.ds(mo(c * 128, 128), 128)
 
     def wo0():
+        loads[4].wait()
         for k in range(4):
             wo[y, k, :, half] = wout_t[:, 128 * k : 128 * k + 128]
         blk = wo.at[y, :, :, half]
@@ -526,6 +543,7 @@
 
     nc = {}
     fa = {}
+    stores = []
 
     def scan_a():
         lane1 = lax.broadcasted_iota(jnp.int32, (1, 128), 1)
@@ -611,7 +629,10 @@
             cols = slice(128 * k, 128 * k + 128)
             lo, hi = 2 * k, 2 * k + 1
             last = jnp.where(rows_first, ecum[255:256, lo : lo + 1], ecum[255:256, hi : hi + 1])
-            fin_out[cols, :] = last * start[cols, :].astype(F32) + dot_tn(wt[:, cols], bc[0])
+            fin[cols, :] = last * start[cols, :].astype(F32) + dot_tn(wt[:, cols], bc[0])
+
+        stores.append(pltpu.make_async_copy(fin, fin_out, ls.at[5]))
+        stores[-1].start()
 
     def nf(j):
         for k in (2 * j, 2 * j + 1):
@@ -693,10 +714,27 @@
         o3[rr, 160:] = (k3[rr] + e2b[rr].astype(F32)).astype(BF16)
         xc[rr, "1bh"] = send(o3.at[rr, pl.ds(160, 160)], e1b.at[rr, pl.ds(160, 160)], xm)
 
+    def ox(rr):
+        zr = m4(z + rr)
+        o2[rr] = out_prod(zr, m4(x + 2)).astype(BF16)
+        xc[rr, "2"] = send(o2.at[rr], e2.at[rr], dev(y, z, m4(x + 2), c))
+        o1[rr] = out_prod(zr, m4(x + 1)).astype(BF16)
+        xc[rr, "1a"] = send(o1.at[rr], e1a.at[rr], xp)
+        o3[rr] = out_prod(zr, m4(x + 3)).astype(BF16)
+        xc[rr, "1b"] = send(o3.at[rr], e1b.at[rr], xm)
+        k0[rr] = out_prod(zr, x)
+
+    def oxe(rr):
+        for k in ("2", "1a", "1b"):
+            xc[rr, k].wait_recv()
+        home(rr, k0[rr] + e1a[rr].astype(F32) + e1b[rr].astype(F32) + e2[rr].astype(F32))
+
     def oe(rr):
         for k in ("1ah", "1bl", "1al", "1bh"):
             xc[rr, k].wait_recv()
-        total = k0[rr] + e1a[rr].astype(F32) + e1b[rr].astype(F32)
+        home(rr, k0[rr] + e1a[rr].astype(F32) + e1b[rr].astype(F32))
+
+    def home(rr, total):
         fs[rr] = total.astype(BF16)
         dst = mt.at[pl.ds(mo(sz * 320, 64), 320), pl.ds(mo(c * 128, 128), 128)]
         cp = copy_of(fs.at[rr], dst, dev(y, m4(z + rr), x, zc), take(), fr_sem + 2 * sz + c)
@@ -724,7 +762,8 @@
                 def _(got=got):
                     got.wait_recv()
 
-        mix_out[...] = mt[...]
+        stores.append(pltpu.make_async_copy(mt, mix_out, ls.at[6]))
+        stores[-1].start()
 
     steps = dict(
         h0=h0,
@@ -740,6 +779,8 @@
         oa=oa,
         od=od,
         oe=oe,
+        ox=ox,
+        oxe=oxe,
         of=of,
         o_far=o_far,
         far_in=far_in,
@@ -756,6 +797,8 @@
         scan_b=scan_b,
         final=final,
         w0=w0,
+        s_pick=s_pick,
+        w_init=w_init,
         wf=wf,
         wg=wg,
         wo0=wo0,
@@ -766,13 +809,11 @@
     loads[0].wait()
     loads[1].wait()
     w_cat()
-    w_init()
-    loads[2].wait()
-    s_pick(1)
-    s_pick(0)
     loads[3].wait()
-    loads[4].wait()
     pl.semaphore_wait(barrier, len(peers))
+    pl.semaphore_signal(tier, inc=1, device_id=zm, device_id_type=MESH)
+    w0(0)
+    h0_near()
 
     for step in ORDER:
         name, *args = step.split()
@@ -780,9 +821,11 @@
 
     for cp in sent:
         cp.finish()
+    for cp in stores:
+        cp.wait()
     for cp in map_copies + direct:
         cp.wait_send()
-    for local, cp in h0_local:
+    for local, _, cp in h0_local:
 
         @pl.when(jnp.logical_not(local))
         def _(cp=cp):
@@ -798,14 +841,22 @@
             cp.wait_send()
 
 
-def finish_body(mixed_t, final, mixed_out, final_out):
-    mixed_out[...] = mixed_t[...].T
-    final_out[...] = final[...]
+def finish_body(mixed_t, final, mixed_out, final_out, mixed, sems):
+    copies = [
+        pltpu.make_async_copy(final, final_out, sems.at[0]),
+        pltpu.make_async_copy(mixed, mixed_out, sems.at[1]),
+    ]
+    copies[0].start()
+    mixed[...] = mixed_t[...].T
+    copies[1].start()
+    for cp in copies:
+        cp.wait()
 
 
 def shards(hidden, snap_map, pool_states, w_zx, w_bc, w_dt, dt_bias, decay_rate, skip, norm_gain, w_out):
     vm = pl.BlockSpec(memory_space=VMEM)
     sm = pl.BlockSpec(memory_space=pltpu.SMEM)
+    hbm = pl.BlockSpec(memory_space=pl.ANY)
     scratch = [
         VMEM((256, 640), BF16),
         VMEM((320, 2, 512), BF16),
@@ -839,17 +890,19 @@
         *[VMEM((4, 160, 128), F32)] * 2,
         *[VMEM((4, 320, 128), BF16)] * 3,
         *[VMEM((4, 160, 128), BF16)] * 2,
-        *[VMEM((4, 320, 128), BF16)] * 3,
+        *[VMEM((4, 320, 128), BF16)] * 4,
         VMEM((640, 256), BF16),
+        VMEM((512, 256), F32),
         pltpu.SemaphoreType.DMA((N_SEM,)),
         pltpu.SemaphoreType.DMA((N_SEM,)),
-        pltpu.SemaphoreType.DMA((5,)),
+        pltpu.SemaphoreType.DMA((7,)),
+        pltpu.SemaphoreType.REGULAR,
     ]
     mixed_t, final = pl.pallas_call(
         body,
         out_shape=(jax.ShapeDtypeStruct((640, 256), BF16), jax.ShapeDtypeStruct((512, 256), F32)),
-        in_specs=[sm] * 4 + [vm] * 2 + [pl.BlockSpec(memory_space=pl.ANY)] * 5,
-        out_specs=(vm, vm),
+        in_specs=[sm] * 4 + [vm] * 2 + [hbm] * 5,
+        out_specs=(hbm, hbm),
         scratch_shapes=scratch,
         compiler_params=pltpu.CompilerParams(
             collective_id=0, has_side_effects=True, vmem_limit_bytes=56 * 1024 * 1024
@@ -871,7 +924,8 @@
         finish_body,
         out_shape=(jax.ShapeDtypeStruct((256, 640), BF16), jax.ShapeDtypeStruct((512, 256), F32)),
         in_specs=[vm, vm],
-        out_specs=(vm, vm),
+        out_specs=(hbm, hbm),
+        scratch_shapes=[VMEM((256, 640), BF16), pltpu.SemaphoreType.DMA((2,))],
     )(mixed_t, final)
     return mixed.reshape(1, 256, 640), final.reshape(1, 8, 64, 256)
 

time: 93.1 us -> 92.3 us (level)
  Pallas kernels: 92.3 us -> 91.3 us
where the time goes in v5:
time: 92.3 us; the launch traced here: 92.1 us
  Pallas kernels  91.3 us (99%)
    pallas_call x1, Pallas kernels, shards(): pl.pallas_call(body, out_shape=(jax.ShapeDtypeStruct((640, 256), BF16), j...  89.3 us
    pallas_call x1, Pallas kernels, shards(): pl.pallas_call(finish_body, out_shape=(jax.ShapeDtypeStruct((256, 640), B...  2.06 us

profile of v5, /device:TPU:1, one launch (start us, length us, event | category | flops | bytes accessed | tf_op | source)
XLA Modules:
  0.0 92.1 jit_solution(2608770319190468667)
XLA Ops:
  0.6 89.3 %shard_map.122 = (bf16[640,256]{1,0:T(8,128)(2,1)}, f32[512,256]{1,0:T(8,128)}) custom-call(s32[16]{0:T(128)} %snap.1, f32[8]{0:T(128)} %bias.1, f32[8]{0:T(128)} %rate.1, f32[8]{0:T(128)} %skip.1, f32[1,512]{1,0:T(1,128)} %bitcast.11, bf16[8,320]{1,0:T(8,128)(2,1)} %bitcast.10, bf16[256,640]{1,0:T(8,128)(2,1)} %bitcast.8, bf16[320,2,512]{2,1,0:T(2,128)(2,1)} %wzx_in.1, ...), custom_call_target="tpu_custom_call" | custom-call | tf_op jit(solution)/shard_map/pallas_call | solution.py:901
  89.9 2.1 %shard_map.123 = (bf16[256,640]{1,0:T(8,128)(2,1)}, f32[512,256]{1,0:T(8,128)}) custom-call(bf16[640,256]{1,0:T(8,128)(2,1)} %get-tuple-element.6.mixed_t, f32[512,256]{1,0:T(8,128)} %get-tuple-element.7.final), custom_call_target="tpu_custom_call" | custom-call | tf_op jit(solution)/shard_map/pallas_call | solution.py:923

commit v6 on v5

--- a/solution.py
+++ b/solution.py
@@ -46,7 +46,6 @@
     "pa 1",
     "s1 0",
     "hg 1",
-    "wo0",
     "hw 1",
     "hf 0",
     "pb1 0",
@@ -55,6 +54,7 @@
     "pb2 1",
     "wg 2",
     "s2 1",
+    "wo0",
     "pa 2",
     "hg 0",
     "hw 0",
@@ -71,11 +71,11 @@
     "scan_a",
     "s4 1",
     "pd 2",
+    "scan_b 0",
+    "scan_b 1",
     "scan_b 2",
-    "scan_b 1",
-    "scan_b 0",
+    "scan_b 3",
     "wog",
-    "scan_b 3",
     "nw",
     "wow",
     "oa 0",
@@ -615,12 +615,16 @@
         upper, under = normed[:128], normed[128:]
         nbuf[z, k, :, half] = jnp.where(c == 0, upper, under)
         ns[k] = jnp.where(c == 0, under, upper)
-        dst = nbuf.at[z, k, :, half]
-        nc[k, "pd"] = send(ns.at[k], dst, dev(y, m4(z + 1), x, 1 - c))
-        nc[k, "md"] = send(ns.at[k], dst, dev(y, m4(z + 3), x, 1 - c))
-        nc[k, "pc"] = send(dst, dst, zp)
-        nc[k, "mc"] = send(dst, dst, zm)
-        nc[k, "s"] = send(ns.at[k], dst, sib)
+        if k % 2 == 0:
+            return
+        j = k // 2
+        both = pl.ds(2 * j, 2)
+        dst = nbuf.at[z, both, :, half]
+        nc[j, "pc"] = send(dst, dst, zp)
+        nc[j, "mc"] = send(dst, dst, zm)
+        nc[j, "pd"] = send(ns.at[both], dst, dev(y, m4(z + 1), x, 1 - c))
+        nc[j, "md"] = send(ns.at[both], dst, dev(y, m4(z + 3), x, 1 - c))
+        nc[j, "s"] = send(ns.at[both], dst, sib)
 
     def final():
         ecum = fa["ecum"]
@@ -635,14 +639,12 @@
         stores[-1].start()
 
     def nf(j):
-        for k in (2 * j, 2 * j + 1):
-            nc[k, "pc"].wait_recv()
-            nc[k, "pd"].wait_recv()
+        nc[j, "pc"].wait_recv()
+        nc[j, "pd"].wait_recv()
         fw = nbuf.at[m4(z + 3), pl.ds(2 * j, 2), pl.ds(0, 64)]
         nc[j, "fp"] = send(fw, fw, zp)
-        for k in (2 * j, 2 * j + 1):
-            nc[k, "mc"].wait_recv()
-            nc[k, "md"].wait_recv()
+        nc[j, "mc"].wait_recv()
+        nc[j, "md"].wait_recv()
         fw = nbuf.at[m4(z + 1), pl.ds(2 * j, 2), pl.ds(64, 64)]
         nc[j, "fm"] = send(fw, fw, zm)
 
@@ -652,8 +654,8 @@
             nc[j, "fm"].wait_recv()
 
     def nw():
-        for k in range(4):
-            nc[k, "s"].wait_recv()
+        for j in range(2):
+            nc[j, "s"].wait_recv()
 
     xc = {}
     fr_sem = take(4)

time: 92.3 us -> 92.7 us (level)
  no operation moved by 1% of the time
where the time goes in v6:
time: 92.7 us; the launch traced here: 92.5 us
  Pallas kernels  91.7 us (99%)
    pallas_call x1, Pallas kernels, shards(): pl.pallas_call(body, out_shape=(jax.ShapeDtypeStruct((640, 256), BF16), j...  89.6 us
    pallas_call x1, Pallas kernels, shards(): pl.pallas_call(finish_body, out_shape=(jax.ShapeDtypeStruct((256, 640), B...  2.06 us

profile of v6, /device:TPU:1, one launch (start us, length us, event | category | flops | bytes accessed | tf_op | source)
XLA Modules:
  0.0 92.5 jit_solution(8597675832916560240)
XLA Ops:
  0.6 89.6 %shard_map.122 = (bf16[640,256]{1,0:T(8,128)(2,1)}, f32[512,256]{1,0:T(8,128)}) custom-call(s32[16]{0:T(128)} %snap.1, f32[8]{0:T(128)} %bias.1, f32[8]{0:T(128)} %rate.1, f32[8]{0:T(128)} %skip.1, f32[1,512]{1,0:T(1,128)} %bitcast.11, bf16[8,320]{1,0:T(8,128)(2,1)} %bitcast.10, bf16[256,640]{1,0:T(8,128)(2,1)} %bitcast.8, bf16[320,2,512]{2,1,0:T(2,128)(2,1)} %wzx_in.1, ...), custom_call_target="tpu_custom_call" | custom-call | tf_op jit(solution)/shard_map/pallas_call | solution.py:903
  90.3 2.1 %shard_map.123 = (bf16[256,640]{1,0:T(8,128)(2,1)}, f32[512,256]{1,0:T(8,128)}) custom-call(bf16[640,256]{1,0:T(8,128)(2,1)} %get-tuple-element.6.mixed_t, f32[512,256]{1,0:T(8,128)} %get-tuple-element.7.final), custom_call_target="tpu_custom_call" | custom-call | tf_op jit(solution)/shard_map/pallas_call | solution.py:925
